TPU v7x, 128 devices: a whole 4x4x4 slice. The times are simulated.
128 devices in a mesh: grp: 4 (over z), shard: 32 (over x, y, core).
Axes of the slice: x: 4, y: 4, z: 4, core: 2. Of those that a mesh axis runs over, the one named last changes fastest.
Arguments:
- queries: float32 [512, 1024], P(('grp', 'shard')), may hold values from -48 to 48
- cache: bfloat16 [524288, 1024], P(('grp', 'shard')), may hold values from -6 to 6
- cand_ids: int32 [512, 256], P(('grp', 'shard')), may hold values from 0 to 524287, as said below
- owner_map: int32 [4096], replicated, may hold values from 0 to 4095, as said below
- teacher_rank: int32 [512, 256], P(('grp', 'shard')), may hold values from 0 to 255, each once within a row
Outputs:
- query_grad: float32 [512, 1024], P(('grp', 'shard'))
- query_loss: float32 [512], P(('grp', 'shard'))
Inputs may be any that keep to these rules, and one draw needn't show every extreme that they name: Passage p of logical block b is cache row owner_map[b] * 128 + p % 128; owner_map is a permutation, and cache rows are split evenly over the devices in mesh order. `cand_ids`: the 1024 candidates of one device's queries lie at most 16 on any one device; a quarter of the devices, the same for every requesting device, hold exactly 16 of every device's candidates.
All inputs are finite; a program needn't handle non-finite values.
Results may differ from a plain program's by a relative error of at most 0.0092.
Values may be sent and summed in bfloat16 or wider, within the bound.
A program may use at most 64 MiB of HBM per device.

v0:
```python
import math

import jax
import jax.numpy as jnp
from jax import lax
from jax.sharding import PartitionSpec as P

BLOCK = 128


def bucket_listwise(raw_scores, member, rank_slots, logit_scale, candidates):
    logits = logit_scale * raw_scores
    top = jnp.max(jnp.where(member, logits, -jnp.inf), axis=(1, 2), keepdims=True)
    shifted = logits - top
    total = jnp.sum(
        jnp.where(member, jnp.exp(jnp.where(member, shifted, 0.0)), 0.0), axis=(1, 2), keepdims=True
    )
    student_log = shifted - jnp.log(total)
    teach = -rank_slots.astype(jnp.float32)[None] * (8.0 / candidates)
    teach_top = jnp.max(jnp.where(member, teach, -jnp.inf), axis=(1, 2), keepdims=True)
    teach = teach - teach_top
    teach_total = jnp.sum(
        jnp.where(member, jnp.exp(jnp.where(member, teach, 0.0)), 0.0), axis=(1, 2), keepdims=True
    )
    teacher_log = teach - jnp.log(teach_total)
    teacher_prob = jnp.exp(teacher_log)
    query_loss = jnp.sum(
        jnp.where(member, teacher_prob * (teacher_log - student_log), 0.0), axis=(1, 2)
    )
    coefficient = jnp.where(
        member, jnp.exp(jnp.where(member, student_log, 0.0)) - teacher_prob, 0.0
    ).astype(jnp.bfloat16)
    return (query_loss, coefficient)


def per_device(queries, cache, cand_ids, owner_map, teacher_rank):
    groups = lax.axis_size("grp")
    shards = lax.axis_size("shard")
    devices = groups * shards
    query_count, feature_width = queries.shape
    candidates = cand_ids.shape[1]
    rows_held = cache.shape[0]
    slot_count = query_count * candidates
    capacity = 2 * slot_count // devices
    logit_scale = 3.0 / math.sqrt(feature_width)
    tile = 128
    tile_count = slot_count // tile
    physical = (jnp.take(owner_map, cand_ids // BLOCK) * BLOCK + cand_ids % BLOCK).reshape(
        slot_count
    )
    owner_dev = physical // rows_held
    local_row = physical % rows_held
    owner_onehot = (
        owner_dev.reshape(tile_count, tile)[:, :, None]
        == jnp.arange(devices, dtype=jnp.int32)[None, None, :]
    ).astype(jnp.float32)
    lower = (
        jnp.arange(tile, dtype=jnp.int32)[:, None] > jnp.arange(tile, dtype=jnp.int32)[None, :]
    ).astype(jnp.float32)
    within = jnp.einsum("ij,bjr->bir", lower, owner_onehot, preferred_element_type=jnp.float32)
    tile_totals = jnp.sum(owner_onehot, axis=1)
    tile_start = jnp.cumsum(tile_totals, axis=0) - tile_totals
    earlier = within + tile_start[:, None, :]
    bucket_pos = jnp.sum(earlier * owner_onehot, axis=2).reshape(slot_count).astype(jnp.int32)
    query_slot = jnp.arange(slot_count, dtype=jnp.int32) // candidates
    packed_values = jnp.stack([local_row, query_slot, teacher_rank.reshape(slot_count)], axis=1)
    empty_slots = jnp.broadcast_to(jnp.array([0, -1, 0], jnp.int32), (devices, capacity, 3))
    packed_slots = empty_slots.at[owner_dev, bucket_pos].set(packed_values)
    requests = packed_slots[:, :, 0]
    slot_query = packed_slots[:, :, 1]
    rank_slots = packed_slots[:, :, 2]
    member = slot_query[None] == jnp.arange(query_count, dtype=jnp.int32)[:, None, None]
    query16 = queries.astype(jnp.bfloat16)
    looked_up = cache[
        lax.all_to_all(requests, ("grp", "shard"), split_axis=0, concat_axis=0, tiled=True)
    ]
    returned = lax.all_to_all(looked_up, ("grp", "shard"), split_axis=0, concat_axis=0, tiled=True)
    raw_scores = jnp.einsum("qd,rcd->qrc", query16, returned, preferred_element_type=jnp.float32)
    query_loss, coefficient = bucket_listwise(
        raw_scores, member, rank_slots, logit_scale, candidates
    )
    query_grad = logit_scale * jnp.einsum(
        "qrc,rcd->qd", coefficient, returned, preferred_element_type=jnp.float32
    )
    query_grad, query_loss = (query_grad, query_loss)
    return (query_grad, query_loss)


def solution(mesh):
    in_specs = (
        P(("grp", "shard"), None),
        P(("grp", "shard"), None),
        P(("grp", "shard"), None),
        P(),
        P(("grp", "shard"), None),
    )
    out_specs = (P(("grp", "shard"), None), P(("grp", "shard")))
    return jax.shard_map(
        per_device, mesh=mesh, in_specs=in_specs, out_specs=out_specs, check_vma=False
    )
```

profile of v0, /device:TPU:1, one launch (start us, length us, event | category | flops | bytes accessed | tf_op | source)
XLA Modules:
  0.0 124.7 jit_solution(16565730969198108952)
XLA Ops:
  0.6 0.0 copy-start
  0.6 0.0 copy-start.5
  0.7 0.0 copy-start.4
  0.7 0.0 copy-start.3
  0.7 0.0 copy-start.2
  0.7 0.7 copy.29
  1.4 0.7 fusion.48
  2.1 0.0 copy-done
  2.1 6.2 %gather_fusion = s32[1024]{0:T(1024)S(1)} fusion(s32[4096]{0:T(1024)S(1)} %copy-done, s32[1024]{0:T(1024)S(1)} %broadcast_clamp_fusion.1), kind=kCustom, calls=%fused_computation | custom fusion | bytes 12288 | tf_op jit(solution)/shard_map/jit(_take)/gather | solution.py:48
  8.3 0.0 copy-done.2
  8.4 0.1 convert_reduce_fusion
  8.6 0.3 fusion.4
  8.9 0.1 and_reduce_fusion
  9.0 0.1 multiply_reduce_fusion
  9.1 0.2 copy.19
  9.4 0.1 broadcast.233
  9.5 3.5 %scatter_fusion = s32[3,2048]{0,1:T(8,128)S(1)} fusion(s32[3,2048]{0,1:T(8,128)S(1)} %broadcast.233, s32[1024]{0:T(1024)S(1)} %broadcast_select_fusion, s32[1024,3]{1,0:T(8,128)S(1)} %copy.19), kind=kCustom, calls=%fused_computation.2 | custom fusion | bytes 40960
  13.0 0.9 copy.20
  13.9 20.9 %all_to_all.17 = s32[128,1,16]{2,1,0:T(1,128)S(1)} all-to-all(s32[128,1,16]{2,1,0:T(1,128)S(1)} %bitcast.60), channel_id=1, replica_groups=mesh['grp'=4,'shard'=32] {'grp','shard'}, dimensions={0} | all-to-all | bytes 16384 | tf_op jit(solution)/shard_map/all_to_all | solution.py:75
  34.9 0.1 reshape.288
  35.0 15.4 %gather_fusion.1 = bf16[2048,1024]{1,0:T(8,128)(2,1)} fusion(bf16[4096,1024]{1,0:T(8,128)(2,1)} %param.7, s32[2048]{0:T(1024)S(1)} %broadcast_clamp_fusion), kind=kCustom, calls=%fused_computation.1 | custom fusion | bytes 8396800 | tf_op jit(solution)/shard_map/gather | solution.py:74
  50.4 5.5 %all-to-all-start.1 = ((bf16[128,16,1024]{2,1,0:T(8,128)(2,1)}), bf16[128,16,1024]{2,1,0:T(8,128)(2,1)}, u32[]{:S(2)}, u32[]{:S(2)}) async-start(bf16[128,16,1024]{2,1,0:T(8,128)(2,1)} %bitcast.56), calls=%async_computation.1 | async-start | bytes 8388608 | tf_op jit(solution)/shard_map/all_to_all | solution.py:77
  55.9 0.1 copy.23
  55.9 0.1 copy.21
  56.0 52.8 %all-to-all-done.1 = bf16[128,16,1024]{2,1,0:T(8,128)(2,1)} async-done(((bf16[128,16,1024]{2,1,0:T(8,128)(2,1)}), bf16[128,16,1024]{2,1,0:T(8,128)(2,1)}, u32[]{:S(2)}, u32[]{:S(2)}) %all-to-all-start.1) | async-done | bytes 4194336 | tf_op jit(solution)/shard_map/all_to_all | solution.py:77
  108.8 7.2 %fusion.39 = f32[128,16,4]{1,2,0:T(4,128)S(1)} fusion(bf16[128,16,1024]{2,1,0:T(8,128)(2,1)} %all-to-all-done.1, f32[4,1024]{1,0:T(4,128)S(1)} %copy-done.1), kind=kOutput, calls=%fused_computation.62 | convolution fusion | flops 16781312 | bytes 4243456 | tf_op jit(solution)/shard_map/qd,rcd->qrc/dot_general | solution.py:78
  116.0 0.1 copy.26
  116.1 0.2 fusion.27
  116.2 0.2 select_reduce_fusion.1
  116.4 0.2 fusion.26
  116.7 0.7 fusion.28
  117.4 7.3 %fusion.8 = f32[4,1024]{1,0:T(4,128)} fusion(bf16[128,16,1024]{2,1,0:T(8,128)(2,1)} %all-to-all-done.1, f32[128,16,4]{0,2,1:T(4,128)S(1)} %copy.26, f32[4]{0:T(128)S(1)} %log.17, f32[4]{0:T(128)S(1)} %get-tuple-element.3, f32[128,16]{0,1:T(8,128)S(1)} %copy.23, f32[4]{0:T(128)S(1)} %log.16, f32[4]{0:T(128)S(1)} %fusion.27, s32[128,16]{0,1:T(8,128)S(1)} %copy.21), kind=kOutput, calls=%fused_computation.10 | convolution fusion | flops 16863232 | bytes 4259904 | tf_op jit(solution)/shard_map/qrc,rcd->qd/dot_general | solution.py:82
  (26 shorter events, 0.2 us)
Async XLA Ops:
  0.6 1.5 %copy-start = (s32[4096]{0:T(1024)S(1)}, s32[4096]{0:T(1024)}, u32[]{:S(2)}) copy-start(s32[4096]{0:T(1024)} %param.9) | copy-start | bytes 49156
  0.6 8.3 %copy-start.5 = (s32[2]{0:T(128)S(1)}, s32[2]{0:T(128)}, u32[]{:S(2)}) copy-start(s32[2]{0:T(128)} %constant.108) | copy-start | bytes 28
  0.7 8.4 %copy-start.4 = (s32[2]{0:T(128)S(1)}, s32[2]{0:T(128)}, u32[]{:S(2)}) copy-start(s32[2]{0:T(128)} %constant.105) | copy-start | bytes 28
  0.7 8.7 %copy-start.3 = (s32[3]{0:T(128)S(1)}, s32[3]{0:T(128)}, u32[]{:S(2)}) copy-start(s32[3]{0:T(128)} %constant.101.clone) | copy-start | bytes 40
  0.7 7.6 %copy-start.2 = (s32[4,256]{1,0:T(4,128)S(1)}, s32[4,256]{1,0:T(4,128)}, u32[]{:S(2)}) copy-start(s32[4,256]{1,0:T(4,128)} %param.8) | copy-start | bytes 12292
  50.4 58.4 %copy-start.1 = (f32[4,1024]{1,0:T(4,128)S(1)}, f32[4,1024]{1,0:T(4,128)}, u32[]{:S(2)}) copy-start(f32[4,1024]{1,0:T(4,128)} %param.6) | copy-start | bytes 49156
  50.4 58.4 %all-to-all-start.1 = ((bf16[128,16,1024]{2,1,0:T(8,128)(2,1)}), bf16[128,16,1024]{2,1,0:T(8,128)(2,1)}, u32[]{:S(2)}, u32[]{:S(2)}) async-start(bf16[128,16,1024]{2,1,0:T(8,128)(2,1)} %bitcast.56), calls=%async_computation.1 | async-start | bytes 8388608 | tf_op jit(solution)/shard_map/all_to_all | solution.py:77
where the time goes:
time: 125 us
  waiting for transfers between devices  52.8 us (42%)
  local copies, waits for them, and re-layouts  27.4 us (22%)
  blocking collectives  20.9 us (17%)
  matrix products  14.7 us (12%)
  starting transfers between devices  5.46 us (4%)
  other arithmetic  2.49 us (2%)
    all_to_all x1, waiting for transfers between devices, per_device(): lax.all_to_all(looked_up, ('grp', 'shard'), split_axis=0, concat_axis=0,...  52.8 us
    all_to_all x1, blocking collectives, per_device(): lax.all_to_all(requests, ('grp', 'shard'), split_axis=0, concat_axis=0, t...  20.9 us
    gather x1, local copies, waits for them, and re-layouts, per_device(): cache[lax.all_to_all(requests, ('grp', 'shard'), split_axis=0, concat_axi...  15.4 us
    dot_general x1, matrix products, per_device(): jnp.einsum('qrc,rcd->qd', coefficient, returned, preferred_element_type=j...  7.28 us
    dot_general x1, matrix products, per_device(): jnp.einsum('qd,rcd->qrc', query16, returned, preferred_element_type=jnp.f...  7.16 us
    gather x2, local copies, waits for them, and re-layouts, per_device(): jnp.take(owner_map, cand_ids // BLOCK) * BLOCK + cand_ids % BLOCK  6.16 us
    all_to_all x1, starting transfers between devices, per_device(): lax.all_to_all(looked_up, ('grp', 'shard'), split_axis=0, concat_axis=0,...  5.46 us
    unnamed x18, local copies, waits for them, and re-layouts  5.26 us
  transfers between devices with their start and end apart: 1, of which 1 were waited for; matrix products, arithmetic and copies ran while one was open for 0% of the time, Pallas kernels for 0%

commit v1 on v0

v1 whole, which is shorter than its diff:
```python
import functools
import math

import jax
import jax.numpy as jnp
from jax import lax
from jax.experimental import pallas as pl
from jax.experimental.pallas import tpu as pltpu
from jax.sharding import PartitionSpec as P

MESH = pl.DeviceIdType.MESH
BLOCK = 128
CAP = 16
NEG = -1e30
F32 = jnp.float32
BF16 = jnp.bfloat16
I32 = jnp.int32


def iota(shape, dim):
    return lax.broadcasted_iota(I32, shape, dim)


def nt(a, b):
    return lax.dot_general(a, b, (((1,), (1,)), ((), ())), preferred_element_type=F32)


def nn(a, b):
    return jnp.dot(a, b, preferred_element_type=F32)


def hot(mask):
    return jnp.where(mask, 1.0, 0.0).astype(BF16)


def col_to_rows(col):
    eye = iota((128, 128), 0) == iota((128, 128), 1)
    rows = [
        jnp.sum(jnp.where(eye, col[k * 128 : (k + 1) * 128], 0.0), axis=0, keepdims=True)
        for k in range(col.shape[0] // 128)
    ]
    return jnp.concatenate(rows, axis=0)


def rows_to_col(rows):
    eye = iota((128, 128), 0) == iota((128, 128), 1)
    cols = [
        jnp.sum(jnp.where(eye, rows[k : k + 1], 0.0), axis=1, keepdims=True)
        for k in range(rows.shape[0])
    ]
    return jnp.concatenate(cols, axis=0)


class Dims:
    def __init__(self, n, queries, cache, cand_ids):
        self.n = n
        self.devices = 2 * n**3
        self.qd, self.width = queries
        self.held = cache[0]
        self.blocks = self.held // BLOCK
        self.cands = cand_ids[1]
        self.rows = self.devices * self.qd
        self.half = self.rows // 2
        self.part = self.half // n
        self.unit = self.part // n
        self.groups = self.devices // 8
        self.grows = 8 * self.qd
        self.stat_rows = self.rows // 128


def kernel(
    d,
    q_ref,
    cand_ref,
    map_ref,
    rank_ref,
    cache_hbm,
    grad_ref,
    loss_ref,
    c_ref,
    qall,
    qpad,
    table,
    ra,
    ra2,
    rb,
    meta,
    nbuf,
    tbuf,
    sbuf,
    cf,
    mbuf,
    dbuf,
    stat,
    sa,
    stat2,
    sb,
    pbuf,
    psend,
    rc1,
    hsend,
    rc2,
    usend,
    rc3,
    asend,
    rc4,
    cache_sem,
    q1s,
    q1r,
    q2s,
    q2r,
    q3s,
    q3r,
    q4s,
    q4r,
    tas,
    tar,
    tbs,
    tbr,
    sas,
    sar,
    sbs,
    sbr,
    r1s,
    r1r,
    r2s,
    r2r,
    r3s,
    r3r,
    r4s,
    r4r,
):
    n = d.n
    z = lax.axis_index("grp")
    shard = lax.axis_index("shard")
    x = shard // (2 * n)
    y = (shard // 2) % n
    c = shard % 2
    scale = 3.0 / math.sqrt(d.width)
    xc = x * 2 + c
    yz = y * n + z
    first = c == 0
    a = jnp.where(first, x, z)
    b = jnp.where(first, z, x)

    def dev(xx, yy, zz, cc):
        return (zz, (xx * n + yy) * 2 + cc)

    def dev_xc(j):
        return dev(j // 2, y, z, j % 2)

    def dev_yz(j):
        return dev(x, j // n, j % n, c)

    def dev_a(j):
        return dev(jnp.where(first, j, x), y, jnp.where(first, z, j), c)

    def dev_b(j):
        return dev(jnp.where(first, x, j), y, jnp.where(first, j, z), c)

    def dev_y(j):
        return dev(x, j, z, c)

    sibling = dev(x, y, z, 1 - c)
    nxc, nyz = 2 * n, n * n

    barrier = pltpu.get_barrier_semaphore()
    for delta in range(1, nxc):
        pl.semaphore_signal(barrier, inc=1, device_id=dev_xc((xc + delta) % nxc), device_id_type=MESH)
    for delta in range(1, nyz):
        pl.semaphore_signal(barrier, inc=1, device_id=dev_yz((yz + delta) % nyz), device_id_type=MESH)

    cache_copy = pltpu.make_async_copy(cache_hbm, c_ref, cache_sem)
    cache_copy.start()

    pending = []

    def send(src, dst, ssem, rsem, to):
        copy = pltpu.make_async_remote_copy(
            src_ref=src, dst_ref=dst, send_sem=ssem, recv_sem=rsem, device_id=to, device_id_type=MESH
        )
        copy.start()
        pending.append(copy)
        return copy

    q16 = q_ref[...]
    pieces = [jnp.where(a == k, q16, 0.0) for k in range(n)]
    qpad[0] = jnp.concatenate(pieces, axis=0).astype(BF16)

    teach = -rank_ref[...].astype(F32) * (8.0 / d.cands)
    teach = teach - jnp.max(teach, axis=1, keepdims=True)
    teacher_log = teach - jnp.log(jnp.sum(jnp.exp(teach), axis=1, keepdims=True))
    prob = jnp.exp(teacher_log)
    entropy = jnp.sum(prob * teacher_log, axis=1, keepdims=True)
    prob_hi = prob.astype(BF16).astype(F32)
    prob_lo = prob - prob_hi

    cand = cand_ref[...]
    blk, off = cand // BLOCK, cand % BLOCK
    omap = map_ref[...]
    map_rows = omap.shape[0]
    halves = jnp.concatenate([omap // 64, omap % 64], axis=0).astype(F32).astype(BF16)
    upper = hot(iota((d.cands, d.cands), 0) < iota((d.cands, d.cands), 1))
    total = jnp.zeros((d.devices, 1), F32)
    acc = jnp.zeros((d.devices, 128), F32)
    for i in range(d.qd):
        bi = blk[i : i + 1]
        low = hot(iota((128, d.cands), 0) == bi % 128)
        got = nn(halves, low)
        high = jnp.where(iota((map_rows, d.cands), 0) == bi // 128, 1.0, 0.0)
        pblk = (
            jnp.sum(got[:map_rows] * high, axis=0, keepdims=True) * 64.0
            + jnp.sum(got[map_rows:] * high, axis=0, keepdims=True)
        ).astype(I32)
        owner, lblk = pblk // d.blocks, pblk % d.blocks
        oz, oshard = owner // (2 * n * n), owner % (2 * n * n)
        place = ((oshard // (2 * n)) * 2 + oshard % 2) * nyz + ((oshard // 2) % n) * n + oz
        mine = jnp.where(iota((d.devices, d.cands), 0) == place, 1.0, 0.0)
        mine16 = mine.astype(BF16)
        earlier = nn(mine16, upper) + total
        pos = jnp.sum(mine * earlier, axis=0, keepdims=True).astype(I32)
        total = total + jnp.sum(mine, axis=1, keepdims=True)
        at = jnp.where(iota((CAP, d.cands), 0) == pos, 1.0, 0.0)
        planes = jnp.concatenate(
            [
                at * lblk.astype(F32),
                at * off[i : i + 1].astype(F32),
                at * float(i),
                at * prob_hi[i : i + 1],
                at * prob_lo[i : i + 1],
                jnp.zeros((128 - 5 * CAP, d.cands), F32),
            ],
            axis=0,
        ).astype(BF16)
        acc = acc + nt(mine16, planes)
    table[...] = acc

    pl.semaphore_wait(barrier, nxc - 1 + nyz - 1)

    for k in range(1, n):
        send(qpad.at[0], qpad.at[k], q1s.at[k], q1r.at[k], dev_a((a + k) % n))
    for k in range(1, nxc):
        j = (xc + k) % nxc
        send(
            table.at[pl.ds(pl.multiple_of(j * nyz, nyz), nyz)],
            ra.at[pl.ds(pl.multiple_of(xc * nyz, nyz), nyz)],
            tas.at[k],
            tar.at[k],
            dev_xc(j),
        )
    own = pl.ds(pl.multiple_of(xc * nyz, nyz), nyz)
    ra[own] = table[own]

    def arrived(dst, rsem):
        pltpu.make_async_remote_copy(
            src_ref=dst, dst_ref=dst, send_sem=rsem, recv_sem=rsem, device_id=sibling, device_id_type=MESH
        ).wait_recv()

    for k in range(1, n):
        arrived(qpad.at[k], q1r.at[k])
    unit_rows = pl.ds(pl.multiple_of(c * d.half + b * d.part + y * d.unit, d.unit), d.unit)
    gathered = qpad[0]
    for k in range(1, n):
        gathered = gathered + qpad[k]
    qall[unit_rows] = gathered
    for k in range(1, n):
        send(qall.at[unit_rows], qall.at[unit_rows], q2s.at[k], q2r.at[k], dev_y((y + k) % n))

    for k in range(1, nxc):
        src = (xc + nxc - k) % nxc
        arrived(ra.at[pl.ds(pl.multiple_of(src * nyz, nyz), nyz)], tar.at[k])
    r, s = iota((d.devices, d.devices), 0), iota((d.devices, d.devices), 1)
    perm = hot((r % nxc) * nyz + r // nxc == s)
    ra2[...] = nn(perm, ra[...].astype(BF16))
    for k in range(1, nyz):
        j = (yz + k) % nyz
        send(
            ra2.at[pl.ds(pl.multiple_of(j * nxc, nxc), nxc)],
            rb.at[pl.ds(pl.multiple_of(yz * nxc, nxc), nxc)],
            tbs.at[k],
            tbr.at[k],
            dev_yz(j),
        )
    own = pl.ds(pl.multiple_of(yz * nxc, nxc), nxc)
    rb[own] = ra2[own]

    for k in range(1, n):
        src = (y + n - k) % n
        rows = pl.ds(pl.multiple_of(c * d.half + b * d.part + src * d.unit, d.unit), d.unit)
        arrived(qall.at[rows], q2r.at[k])
    part_rows = pl.ds(pl.multiple_of(c * d.half + b * d.part, d.part), d.part)
    for k in range(1, n):
        send(qall.at[part_rows], qall.at[part_rows], q3s.at[k], q3r.at[k], dev_b((b + k) % n))

    for k in range(1, nyz):
        src = (yz + nyz - k) % nyz
        arrived(rb.at[pl.ds(pl.multiple_of(src * nxc, nxc), nxc)], tbr.at[k])
    pc, pb, py, pa = r // n**3, (r // n**2) % n, (r // n) % n, r % n
    px, pz = jnp.where(pc == 0, pa, pb), jnp.where(pc == 0, pb, pa)
    perm = hot(((py * n + pz) * n + px) * 2 + pc == s)
    lists = nn(perm, rb[...].astype(BF16)).astype(BF16)
    lane = iota((128, 128), 1)
    sub = iota((128, 128), 0)
    pick = jnp.where(iota((d.devices, 128), 0) % 8 == iota((d.devices, 128), 1) // CAP, 1.0, 0.0)
    for p in range(5):
        spread = nn(lists, hot(sub == p * CAP + lane % CAP)) * pick
        meta[p] = jnp.sum(spread.reshape(d.groups, 8, 128), axis=1)

    def fill(g, _):
        lb, lo, lq, hi, low = [meta[p, pl.ds(g, 1), :] for p in range(5)]
        key = lb.astype(I32) * d.grows + (iota((1, 128), 1) // CAP) * d.qd + lq.astype(I32)
        same = iota((128, 128), 0) == lo.astype(I32)
        zero = jnp.zeros((128, 128), F32)
        right = jnp.concatenate(
            [
                jnp.concatenate([jnp.where(same & (hi > 0.0), 1.0, 0.0), zero], axis=1),
                jnp.concatenate([jnp.where(same, hi, 0.0), jnp.where(same, low, 0.0)], axis=1),
            ],
            axis=0,
        ).astype(BF16)
        step = max(1, 256 // d.grows)
        for c0 in range(0, d.blocks, step):
            left = hot(iota((step * d.grows, 128), 0) + c0 * d.grows == key)
            out = nt(jnp.concatenate([left, left], axis=1), right)
            rows = pl.ds(pl.multiple_of(g * d.grows, d.grows), d.grows)
            for k in range(step):
                cols = slice((c0 + k) * 128, (c0 + k + 1) * 128)
                nbuf[rows, cols] = out[k * d.grows : (k + 1) * d.grows, :128]
                tbuf[rows, cols] = out[k * d.grows : (k + 1) * d.grows, 128:]
        return 0

    lax.fori_loop(0, d.groups, fill, 0)

    for k in range(1, n):
        src = (b + n - k) % n
        rows = pl.ds(pl.multiple_of(c * d.half + src * d.part, d.part), d.part)
        arrived(qall.at[rows], q3r.at[k])
    half_rows = pl.ds(pl.multiple_of(c * d.half, d.half), d.half)
    other_rows = pl.ds(pl.multiple_of((1 - c) * d.half, d.half), d.half)
    send(qall.at[half_rows], qall.at[half_rows], q4s.at[0], q4r.at[0], sibling)
    cache_copy.wait()
    arrived(qall.at[other_rows], q4r.at[0])

    mbuf[...] = jnp.full(mbuf.shape, NEG, F32)
    dbuf[...] = jnp.zeros(dbuf.shape, F32)
    tile = 256

    def score(t, _):
        cols = pl.ds(pl.multiple_of(t * tile, tile), tile)
        logits = nt(qall[...], c_ref[cols, :]) * scale
        dd = tbuf[:, cols] * logits
        logits = jnp.where(nbuf[:, cols] > 0.0, logits, NEG)
        sbuf[:, cols] = logits
        mbuf[...] = jnp.maximum(mbuf[...], jnp.maximum(logits[:, :128], logits[:, 128:]))
        dbuf[...] += dd[:, :128] + dd[:, 128:]
        return 0

    lax.fori_loop(0, d.held // tile, score, 0)
    top = jnp.max(mbuf[...], axis=1, keepdims=True)
    dot_t = jnp.sum(dbuf[...], axis=1, keepdims=True)
    dbuf[...] = jnp.zeros(dbuf.shape, F32)
    mbuf[...] = jnp.broadcast_to(top, mbuf.shape)

    def expo(t, _):
        cols = pl.ds(pl.multiple_of(t * 128, 128), 128)
        e = nbuf[:, cols] * jnp.exp(sbuf[:, cols] - mbuf[...])
        sbuf[:, cols] = e
        dbuf[...] += e
        return 0

    lax.fori_loop(0, d.held // 128, expo, 0)
    total = jnp.sum(dbuf[...], axis=1, keepdims=True)

    nr = d.stat_rows
    my_top = col_to_rows(top)
    packed = [my_top, col_to_rows(total), col_to_rows(dot_t)]
    if 16 - 3 * nr:
        packed.append(jnp.zeros((16 - 3 * nr, 128), F32))
    stat[...] = jnp.concatenate(packed, axis=0)

    def combine(pieces):
        tops = [p[:nr] for p in pieces]
        best = functools.reduce(jnp.maximum, tops)
        zs = sum(p[nr : 2 * nr] * jnp.exp(t - best) for p, t in zip(pieces, tops))
        ds = sum(p[2 * nr : 3 * nr] for p in pieces)
        return best, zs, ds

    for k in range(1, nxc):
        send(stat, sa.at[k], sas.at[k], sar.at[k], dev_xc((xc + k) % nxc))
    for k in range(1, nxc):
        arrived(sa.at[k], sar.at[k])
    packed = list(combine([stat[...]] + [sa[k] for k in range(1, nxc)]))
    if 16 - 3 * nr:
        packed.append(jnp.zeros((16 - 3 * nr, 128), F32))
    stat2[...] = jnp.concatenate(packed, axis=0)
    for k in range(1, nyz):
        send(stat2, sb.at[k], sbs.at[k], sbr.at[k], dev_yz((yz + k) % nyz))
    for k in range(1, nyz):
        arrived(sb.at[k], sbr.at[k])
    best, zs, ds = combine([stat2[...]] + [sb[k] for k in range(1, nyz)])

    losses = best + jnp.log(zs) - ds
    flat = iota((nr, 128), 0) * 128 + iota((nr, 128), 1)
    row0 = c * d.half + b * d.part + y * d.unit + a * d.qd
    out = jnp.zeros((1, 128), F32)
    for i in range(d.qd):
        value = jnp.sum(
            jnp.sum(jnp.where(flat == row0 + i, losses, 0.0), axis=0, keepdims=True), axis=1, keepdims=True
        )
        out = jnp.where(iota((1, 128), 1) == i, value + entropy[i : i + 1], out)
    loss_ref[...] = out[:, : d.qd]

    mbuf[...] = jnp.broadcast_to(rows_to_col(jnp.exp(my_top - best) / zs), mbuf.shape)

    def coef(t, _):
        cols = pl.ds(pl.multiple_of(t * 128, 128), 128)
        cf[:, cols] = (sbuf[:, cols] * mbuf[...] - tbuf[:, cols]).astype(BF16)
        return 0

    lax.fori_loop(0, d.held // 128, coef, 0)

    for t in range(d.width // 256):
        cols = slice(t * 256, (t + 1) * 256)
        got = nn(cf[...], c_ref[:, cols]) * scale
        pbuf[:, cols] = got
        psend[:, cols] = got.astype(BF16)

    send(psend.at[other_rows], rc1, r1s.at[0], r1r.at[0], sibling)
    arrived(rc1, r1r.at[0])
    pbuf[half_rows] = pbuf[half_rows] + rc1[...].astype(F32)
    hsend[...] = pbuf[half_rows].astype(BF16)
    for k in range(1, n):
        j = (b + k) % n
        send(
            hsend.at[pl.ds(pl.multiple_of(j * d.part, d.part), d.part)],
            rc2.at[k],
            r2s.at[k],
            r2r.at[k],
            dev_b(j),
        )
    for k in range(1, n):
        arrived(rc2.at[k], r2r.at[k])
    part = pbuf[part_rows]
    for k in range(1, n):
        part = part + rc2[k].astype(F32)
    pbuf[part_rows] = part
    usend[...] = part.astype(BF16)
    for k in range(1, n):
        j = (y + k) % n
        send(
            usend.at[pl.ds(pl.multiple_of(j * d.unit, d.unit), d.unit)],
            rc3.at[k],
            r3s.at[k],
            r3r.at[k],
            dev_y(j),
        )
    for k in range(1, n):
        arrived(rc3.at[k], r3r.at[k])
    unit = pbuf[unit_rows]
    for k in range(1, n):
        unit = unit + rc3[k].astype(F32)
    for k in range(n):
        asend[k, : d.qd] = unit[k * d.qd : (k + 1) * d.qd]
    for k in range(1, n):
        j = (a + k) % n
        send(asend.at[j], rc4.at[k], r4s.at[k], r4r.at[k], dev_a(j))
    mine = asend[a]
    for k in range(1, n):
        arrived(rc4.at[k], r4r.at[k])
    for k in range(1, n):
        mine = mine + rc4[k]
    grad_ref[...] = mine[: d.qd]

    for copy in pending:
        copy.wait_send()


def per_device(n, queries, cache, cand_ids, owner_map, teacher_rank):
    d = Dims(n, queries.shape, cache.shape, cand_ids.shape)
    w = d.width
    nxc, nyz = 2 * n, n * n
    dma = lambda k: [pltpu.SemaphoreType.DMA((k,))] * 2
    vmem = pl.BlockSpec(memory_space=pltpu.VMEM)
    grad, loss = pl.pallas_call(
        functools.partial(kernel, d),
        out_shape=(
            jax.ShapeDtypeStruct((d.qd, w), F32),
            jax.ShapeDtypeStruct((1, d.qd), F32),
        ),
        in_specs=[vmem] * 4 + [pl.BlockSpec(memory_space=pl.ANY)],
        out_specs=(vmem, vmem),
        scratch_shapes=[
            pltpu.VMEM((d.held, w), BF16),
            pltpu.VMEM((d.rows, w), BF16),
            pltpu.VMEM((n, d.unit, w), BF16),
            pltpu.VMEM((d.devices, 128), F32),
            pltpu.VMEM((d.devices, 128), F32),
            pltpu.VMEM((d.devices, 128), F32),
            pltpu.VMEM((d.devices, 128), F32),
            pltpu.VMEM((5, d.groups, 128), F32),
            pltpu.VMEM((d.rows, d.held), F32),
            pltpu.VMEM((d.rows, d.held), F32),
            pltpu.VMEM((d.rows, d.held), F32),
            pltpu.VMEM((d.rows, d.held), BF16),
            pltpu.VMEM((d.rows, 128), F32),
            pltpu.VMEM((d.rows, 128), F32),
            pltpu.VMEM((16, 128), F32),
            pltpu.VMEM((nxc, 16, 128), F32),
            pltpu.VMEM((16, 128), F32),
            pltpu.VMEM((nyz, 16, 128), F32),
            pltpu.VMEM((d.rows, w), F32),
            pltpu.VMEM((d.rows, w), BF16),
            pltpu.VMEM((d.half, w), BF16),
            pltpu.VMEM((d.half, w), BF16),
            pltpu.VMEM((n, d.part, w), BF16),
            pltpu.VMEM((d.part, w), BF16),
            pltpu.VMEM((n, d.unit, w), BF16),
            pltpu.VMEM((n, 8, w), F32),
            pltpu.VMEM((n, 8, w), F32),
            pltpu.SemaphoreType.DMA,
            *dma(n),
            *dma(n),
            *dma(n),
            *dma(1),
            *dma(nxc),
            *dma(nyz),
            *dma(nxc),
            *dma(nyz),
            *dma(1),
            *dma(n),
            *dma(n),
            *dma(n),
        ],
        compiler_params=pltpu.CompilerParams(
            collective_id=0, has_side_effects=True, vmem_limit_bytes=58 * 2**20
        ),
    )(queries, cand_ids, owner_map.reshape(-1, 128), teacher_rank, cache)
    return grad, loss.reshape(d.qd)


def solution(mesh):
    n = mesh.shape["grp"]
    both = P(("grp", "shard"), None)
    return jax.shard_map(
        functools.partial(per_device, n),
        mesh=mesh,
        in_specs=(both, both, both, P(), both),
        out_specs=(both, P(("grp", "shard"))),
        check_vma=False,
    )
```

time: 125 us -> 74.3 us (0.59)
  Pallas kernels: 0 us -> 70.9 us
  waiting for transfers between devices: 52.8 us -> 0 us
  local copies, waits for them, and re-layouts: 27.4 us -> 2.46 us
  blocking collectives: 20.9 us -> 0 us
  matrix products: 14.7 us -> 0 us
  starting transfers between devices: 5.46 us -> 0 us
  other arithmetic: 2.49 us -> 0 us
    pallas_call x0 -> x1, Pallas kernels: none -> 70.9 us  [per_device(): pl.pallas_call(functools.partial(kernel, d), out_shape=(jax.ShapeDtypeStr...]
    all_to_all x1 -> x0, waiting for transfers between devices: 52.8 us -> none  [per_device(): lax.all_to_all(looked_up, ('grp', 'shard'), split_axis=0, concat_axis=0,...]
    gather x3 -> x0, local copies, waits for them, and re-layouts: 21.6 us -> none  [the longest x1 15.4 us: per_device(): cache[lax.all_to_all(requests, ('grp', 'shard'), split_axis=0, concat_axi...]
    all_to_all x1 -> x0, blocking collectives: 20.9 us -> none  [per_device(): lax.all_to_all(requests, ('grp', 'shard'), split_axis=0, concat_axis=0, t...]
    dot_general x3 -> x0, matrix products: 14.7 us -> none  [the longest x1 7.28 us: per_device(): jnp.einsum('qrc,rcd->qd', coefficient, returned, preferred_element_type=j...]
    all_to_all x1 -> x0, starting transfers between devices: 5.46 us -> none  [per_device(): lax.all_to_all(looked_up, ('grp', 'shard'), split_axis=0, concat_axis=0,...]
    unnamed x18 -> x2, local copies, waits for them, and re-layouts: 5.26 us -> 2.46 us
    reduce_sum x4 -> x0, other arithmetic: 1.3 us -> none  [the longest x1 0.73 us: bucket_listwise(): jnp.sum(jnp.where(member, teacher_prob * (teacher_log - student_log), 0.0...]
  transfers between devices with their start and end apart: 1 -> 0, of which waited for: 1 -> 0; matrix products, arithmetic and copies ran while one was open for 0% -> 0% of each run, Pallas kernels for 0% -> 0%
where the time goes in v1:
time: 74.3 us; the launch traced here: 74 us
  Pallas kernels  70.9 us (95%)
  local copies, waits for them, and re-layouts  2.46 us (3%)
    pallas_call x1, Pallas kernels, per_device(): pl.pallas_call(functools.partial(kernel, d), out_shape=(jax.ShapeDtypeStr...  70.9 us
    unnamed x2, local copies, waits for them, and re-layouts  2.46 us

profile of v1, /device:TPU:1, one launch (start us, length us, event | category | flops | bytes accessed | tf_op | source)
XLA Modules:
  0.0 74.0 jit_solution(5741475075746045302)
XLA Ops:
  0.6 70.9 %shard_map.68 = (f32[4,1024]{1,0:T(4,128)}, f32[1,4]{1,0:T(1,128)}) custom-call(f32[4,1024]{1,0:T(4,128)} %q_ref.1, s32[4,256]{1,0:T(4,128)} %cand_ref.1, s32[32,128]{1,0:T(8,128)} %bitcast.2, s32[4,256]{1,0:T(4,128)} %rank_ref.1, bf16[4096,1024]{1,0:T(8,128)(2,1)} %cache_hbm.1), custom_call_target="tpu_custom_call" | custom-call | tf_op jit(solution)/shard_map/pallas_call | solution.py:484
  71.6 1.3 %copy.9 = f32[4,1024]{1,0:T(4,128)} copy(f32[4,1024]{1,0:T(4,128)} %get-tuple-element.8) | data formatting | bytes 32768
  72.9 1.1 %copy.10 = f32[4]{0:T(128)} copy(f32[4]{0:T(128)} %bitcast.3) | data formatting | bytes 32

commit v2 on v1

v2 whole, which is shorter than its diff:
```python
import functools
import math

import jax
import jax.numpy as jnp
from jax import lax
from jax.experimental import pallas as pl
from jax.experimental.pallas import tpu as pltpu
from jax.sharding import PartitionSpec as P

MESH = pl.DeviceIdType.MESH
BLOCK = 128
CAP = 16
CUTS = 2
NEG = -1e30
F32 = jnp.float32
BF16 = jnp.bfloat16
I32 = jnp.int32


def iota(shape, dim):
    return lax.broadcasted_iota(I32, shape, dim)


def nt(a, b):
    return lax.dot_general(a, b, (((1,), (1,)), ((), ())), preferred_element_type=F32)


def nn(a, b):
    return jnp.dot(a, b, preferred_element_type=F32)


def hot(mask):
    return jnp.where(mask, 1.0, 0.0).astype(BF16)


def col_to_rows(col):
    eye = iota((128, 128), 0) == iota((128, 128), 1)
    rows = [
        jnp.sum(jnp.where(eye, col[k * 128 : (k + 1) * 128], 0.0), axis=0, keepdims=True)
        for k in range(col.shape[0] // 128)
    ]
    return jnp.concatenate(rows, axis=0)


def rows_to_col(rows):
    eye = iota((128, 128), 0) == iota((128, 128), 1)
    cols = [
        jnp.sum(jnp.where(eye, rows[k : k + 1], 0.0), axis=1, keepdims=True)
        for k in range(rows.shape[0])
    ]
    return jnp.concatenate(cols, axis=0)


class Dims:
    def __init__(self, n, queries, cache, cand_ids):
        self.n = n
        self.chips = n**3
        self.devices = 2 * self.chips
        self.qd, self.width = queries
        self.held = cache[0]
        self.blocks = self.held // BLOCK
        self.cands = cand_ids[1]
        self.rows = self.devices * self.qd
        self.half = self.rows // 2
        self.groups = self.devices // 8
        self.grows = 8 * self.qd
        self.stat_rows = self.rows // 128
        self.layer = n * n
        self.tile = min(1024, self.held)
        self.cut = self.width // CUTS


def kernel(
    d,
    q_ref,
    cand_ref,
    map_ref,
    rank_ref,
    cache_hbm,
    grad_ref,
    loss_ref,
    c_ref,
    qown,
    qrecv,
    qall,
    table,
    ra,
    ra2,
    rb,
    meta,
    nbuf,
    tbuf,
    sbuf,
    et,
    mbuf,
    zbuf,
    dbuf,
    stat,
    sa,
    stat2,
    sb,
    uv,
    csend,
    crecv,
    psend,
    precv,
    cache_sem,
    qs,
    qr,
    xs,
    xr,
    tas,
    tar,
    tbs,
    tbr,
    sas,
    sar,
    sbs,
    sbr,
    cs,
    cr,
    ps,
    pr,
):
    n = d.n
    z = lax.axis_index("grp")
    shard = lax.axis_index("shard")
    x = shard // (2 * n)
    y = (shard // 2) % n
    c = shard % 2
    scale = 3.0 / math.sqrt(d.width)
    xc = x * 2 + c
    yz = y * n + z
    chip = z * d.layer + shard // 2
    nxc, nyz = 2 * n, n * n

    def dev(xx, yy, zz, cc):
        return (zz, (xx * n + yy) * 2 + cc)

    def dev_xc(j):
        return dev(j // 2, y, z, j % 2)

    def dev_yz(j):
        return dev(x, j // n, j % n, c)

    def dev_chip(h):
        return (h // d.layer, (h % d.layer) * 2 + c)

    sibling = dev(x, y, z, 1 - c)

    barrier = pltpu.get_barrier_semaphore()

    def greet(k, _):
        pl.semaphore_signal(
            barrier, inc=1, device_id=dev_chip((chip + k) % d.chips), device_id_type=MESH
        )
        return 0

    lax.fori_loop(1, d.chips, greet, 0)
    other_core = 0
    for k in range(1, nxc):
        if k % 2:
            other_core += 1
            pl.semaphore_signal(barrier, inc=1, device_id=dev_xc((xc + k) % nxc), device_id_type=MESH)

    cache_copy = pltpu.make_async_copy(cache_hbm, c_ref, cache_sem)
    cache_copy.start()

    pending = []

    def remote(src, dst, ssem, rsem, to):
        return pltpu.make_async_remote_copy(
            src_ref=src, dst_ref=dst, send_sem=ssem, recv_sem=rsem, device_id=to, device_id_type=MESH
        )

    def send(src, dst, ssem, rsem, to):
        copy = remote(src, dst, ssem, rsem, to)
        copy.start()
        pending.append(copy)

    def arrived(dst, rsem):
        remote(dst, dst, rsem, rsem, sibling).wait_recv()

    def sent(src, ssem):
        remote(src, src, ssem, ssem, sibling).wait_send()

    q16 = q_ref[...].astype(BF16)
    qown[...] = q16
    qrecv[chip] = q16

    teach = -rank_ref[...].astype(F32) * (8.0 / d.cands)
    teach = teach - jnp.max(teach, axis=1, keepdims=True)
    teacher_log = teach - jnp.log(jnp.sum(jnp.exp(teach), axis=1, keepdims=True))
    prob = jnp.exp(teacher_log)
    entropy = jnp.sum(prob * teacher_log, axis=1, keepdims=True)
    prob_hi = prob.astype(BF16).astype(F32)
    prob_lo = prob - prob_hi

    cand = cand_ref[...]
    blk, off = cand // BLOCK, cand % BLOCK
    omap = map_ref[...]
    map_rows = omap.shape[0]
    halves = jnp.concatenate([omap // 64, omap % 64], axis=0).astype(F32).astype(BF16)
    upper = hot(iota((d.cands, d.cands), 0) < iota((d.cands, d.cands), 1))
    total = jnp.zeros((d.devices, 1), F32)
    acc = jnp.zeros((d.devices, 128), F32)
    for i in range(d.qd):
        bi = blk[i : i + 1]
        low = hot(iota((128, d.cands), 0) == bi % 128)
        got = nn(halves, low)
        high = jnp.where(iota((map_rows, d.cands), 0) == bi // 128, 1.0, 0.0)
        pblk = (
            jnp.sum(got[:map_rows] * high, axis=0, keepdims=True) * 64.0
            + jnp.sum(got[map_rows:] * high, axis=0, keepdims=True)
        ).astype(I32)
        owner, lblk = pblk // d.blocks, pblk % d.blocks
        oz, oshard = owner // (2 * n * n), owner % (2 * n * n)
        place = ((oshard // (2 * n)) * 2 + oshard % 2) * nyz + ((oshard // 2) % n) * n + oz
        mine = jnp.where(iota((d.devices, d.cands), 0) == place, 1.0, 0.0)
        mine16 = mine.astype(BF16)
        earlier = nn(mine16, upper) + total
        pos = jnp.sum(mine * earlier, axis=0, keepdims=True).astype(I32)
        total = total + jnp.sum(mine, axis=1, keepdims=True)
        at = jnp.where(iota((CAP, d.cands), 0) == pos, 1.0, 0.0)
        planes = jnp.concatenate(
            [
                at * lblk.astype(F32),
                at * off[i : i + 1].astype(F32),
                at * float(i),
                at * prob_hi[i : i + 1],
                at * prob_lo[i : i + 1],
                jnp.zeros((128 - 5 * CAP, d.cands), F32),
            ],
            axis=0,
        ).astype(BF16)
        acc = acc + nt(mine16, planes)
    table[...] = acc

    pl.semaphore_wait(barrier, d.chips - 1 + other_core)

    for k in range(1, nxc):
        j = (xc + k) % nxc
        send(
            table.at[pl.ds(pl.multiple_of(j * nyz, nyz), nyz)],
            ra.at[pl.ds(pl.multiple_of(xc * nyz, nyz), nyz)],
            tas.at[k],
            tar.at[k],
            dev_xc(j),
        )

    def give(k, _):
        remote(qown, qrecv.at[chip], qs.at[0], qr.at[z], dev_chip((chip + k) % d.chips)).start()
        return 0

    lax.fori_loop(1, d.chips, give, 0)
    own = pl.ds(pl.multiple_of(xc * nyz, nyz), nyz)
    ra[own] = table[own]
    for k in range(1, nxc):
        src = (xc + nxc - k) % nxc
        arrived(ra.at[pl.ds(pl.multiple_of(src * nyz, nyz), nyz)], tar.at[k])

    r, s = iota((d.devices, d.devices), 0), iota((d.devices, d.devices), 1)
    perm = hot((r % nxc) * nyz + r // nxc == s)
    ra2[...] = nn(perm, ra[...].astype(BF16))
    for k in range(1, nyz):
        j = (yz + k) % nyz
        send(
            ra2.at[pl.ds(pl.multiple_of(j * nxc, nxc), nxc)],
            rb.at[pl.ds(pl.multiple_of(yz * nxc, nxc), nxc)],
            tbs.at[k],
            tbr.at[k],
            dev_yz(j),
        )
    own = pl.ds(pl.multiple_of(yz * nxc, nxc), nxc)
    rb[own] = ra2[own]
    for k in range(1, nyz):
        src = (yz + nyz - k) % nyz
        arrived(rb.at[pl.ds(pl.multiple_of(src * nxc, nxc), nxc)], tbr.at[k])

    rc = jnp.where(r < d.chips, c, 1 - c)
    rh = r % d.chips
    rz, rx, ry = rh // d.layer, (rh // n) % n, rh % n
    perm = hot(((ry * n + rz) * n + rx) * 2 + rc == s)
    lists = nn(perm, rb[...].astype(BF16)).astype(BF16)
    lane = iota((128, 128), 1)
    sub = iota((128, 128), 0)
    pick = jnp.where(iota((d.devices, 128), 0) % 8 == iota((d.devices, 128), 1) // CAP, 1.0, 0.0)
    for p in range(5):
        spread = nn(lists, hot(sub == p * CAP + lane % CAP)) * pick
        meta[p] = jnp.sum(spread.reshape(d.groups, 8, 128), axis=1)

    def fill(g, _):
        lb, lo, lq, hi, low = [meta[p, pl.ds(g, 1), :] for p in range(5)]
        key = lb.astype(I32) * d.grows + (iota((1, 128), 1) // CAP) * d.qd + lq.astype(I32)
        same = iota((128, 128), 0) == lo.astype(I32)
        zero = jnp.zeros((128, 128), F32)
        right = jnp.concatenate(
            [
                jnp.concatenate([jnp.where(same & (hi > 0.0), 1.0, 0.0), zero], axis=1),
                jnp.concatenate([jnp.where(same, hi, 0.0), jnp.where(same, low, 0.0)], axis=1),
            ],
            axis=0,
        ).astype(BF16)
        step = max(1, 256 // d.grows)
        for c0 in range(0, d.blocks, step):
            left = hot(iota((step * d.grows, 128), 0) + c0 * d.grows == key)
            out = nt(jnp.concatenate([left, left], axis=1), right)
            rows = pl.ds(pl.multiple_of(g * d.grows, d.grows), d.grows)
            for k in range(step):
                cols = slice((c0 + k) * 128, (c0 + k + 1) * 128)
                nbuf[rows, cols] = out[k * d.grows : (k + 1) * d.grows, :128]
                tp = out[k * d.grows : (k + 1) * d.grows, 128:]
                tbuf[rows, cols] = tp
                et[pl.ds(pl.multiple_of(d.rows + g * d.grows, d.grows), d.grows), cols] = tp.astype(BF16)
        return 0

    lax.fori_loop(0, d.groups, fill, 0)

    per = max(1, 16 // d.qd)
    for k in range(n):
        layer = (z + k) % n
        count = d.layer - 1 if k == 0 else d.layer
        arrived(qrecv.at[pl.ds(layer * d.layer, count)], qr.at[layer])
        for i in range(0, d.layer, per):
            rows = [qrecv[layer * d.layer + i + j].astype(F32) for j in range(per)]
            at = pl.multiple_of((layer * d.layer + i) * d.qd, per * d.qd)
            qall[pl.ds(at, per * d.qd)] = jnp.concatenate(rows, axis=0).astype(BF16)
        size = d.layer * d.qd
        here = pl.ds(pl.multiple_of(layer * size, size), size)
        there = pl.ds(pl.multiple_of(d.half + layer * size, size), size)
        send(qall.at[here], qall.at[there], xs.at[k], xr.at[layer], sibling)
    cache_copy.wait()
    cache_waited = True

    mbuf[...] = jnp.full(mbuf.shape, NEG, F32)
    zbuf[...] = jnp.zeros(zbuf.shape, F32)
    dbuf[...] = jnp.zeros(dbuf.shape, F32)
    halves = [slice(0, d.half), slice(d.half, d.rows)]

    def score(rows, cols):
        raw = nt(qall[rows], c_ref[cols, :])
        raw = jnp.where(nbuf[rows, cols] > 0.0, raw, NEG)
        sbuf[rows, cols] = raw
        best = mbuf[rows]
        for k in range(d.tile // 128):
            best = jnp.maximum(best, raw[:, k * 128 : (k + 1) * 128])
        mbuf[rows] = best

    def expo(rows, t):
        step = min(64, d.half)
        for r0 in range(rows.start, rows.stop, step):
            rr = slice(r0, r0 + step)
            top = mbuf[rr]
            za, da = zbuf[rr], dbuf[rr]
            for k in range(d.tile // 128):
                cols = pl.ds(pl.multiple_of(t * d.tile + k * 128, 128), 128)
                raw = sbuf[rr, cols]
                e = nbuf[rr, cols] * jnp.exp((raw - top) * scale)
                et[rr, cols] = e.astype(BF16)
                za = za + e
                da = da + tbuf[rr, cols] * raw
            zbuf[rr], dbuf[rr] = za, da

    def widest(rows):
        mbuf[rows] = jnp.broadcast_to(jnp.max(mbuf[rows], axis=1, keepdims=True), (d.half, 128))

    def tiles(body):
        def step(t, _):
            body(t, pl.ds(pl.multiple_of(t * d.tile, d.tile), d.tile))
            return 0

        lax.fori_loop(0, d.held // d.tile, step, 0)

    tiles(lambda t, cols: score(halves[0], cols))
    widest(halves[0])
    for layer in range(n):
        size = d.layer * d.qd
        arrived(qall.at[pl.ds(d.half + layer * size, size)], xr.at[layer])

    def both(t, cols):
        score(halves[1], cols)
        expo(halves[0], t)

    tiles(both)
    widest(halves[1])
    tiles(lambda t, cols: expo(halves[1], t))

    nr = d.stat_rows
    my_top = col_to_rows(mbuf[:, :1]) * scale
    packed = [
        my_top,
        col_to_rows(jnp.sum(zbuf[...], axis=1, keepdims=True)),
        col_to_rows(jnp.sum(dbuf[...], axis=1, keepdims=True)) * scale,
    ]
    spare = [jnp.zeros((16 - 3 * nr, 128), F32)] if 16 - 3 * nr else []
    stat[...] = jnp.concatenate(packed + spare, axis=0)

    def swap(v):
        return jnp.concatenate([v[nr // 2 :], v[: nr // 2]], axis=0)

    def combine(pieces):
        tops = [p[0] for p in pieces]
        best = functools.reduce(jnp.maximum, tops)
        zs = sum(p[1] * jnp.exp(t - best) for p, t in zip(pieces, tops))
        ds = sum(p[2] for p in pieces)
        return best, zs, ds

    def three(v):
        return [v[:nr], v[nr : 2 * nr], v[2 * nr : 3 * nr]]

    for k in range(1, nxc):
        send(stat, sa.at[k], sas.at[k], sar.at[k], dev_xc((xc + k) % nxc))

    uv_cols = 256

    def product(t, _):
        cols = pl.ds(pl.multiple_of(t * uv_cols, uv_cols), uv_cols)
        uv[:, cols] = nn(et[...], c_ref[:, cols])
        return 0

    steps = d.width // uv_cols
    lax.fori_loop(0, steps // 2, product, 0)
    for k in range(1, nxc):
        arrived(sa.at[k], sar.at[k])
    pieces = [three(stat[...])]
    for k in range(1, nxc):
        got = three(sa[k])
        pieces.append([swap(v) for v in got] if k % 2 else got)
    stat2[...] = jnp.concatenate(list(combine(pieces)) + spare, axis=0)
    for k in range(1, nyz):
        send(stat2, sb.at[k], sbs.at[k], sbr.at[k], dev_yz((yz + k) % nyz))
    lax.fori_loop(steps // 2, steps, product, 0)
    for k in range(1, nyz):
        arrived(sb.at[k], sbr.at[k])
    best, zs, ds = combine([three(stat2[...])] + [three(sb[k]) for k in range(1, nyz)])

    zbuf[...] = jnp.broadcast_to(rows_to_col(scale * jnp.exp(my_top - best) / zs), zbuf.shape)

    def part(rows, cols):
        wide = jnp.concatenate([zbuf[rows]] * (d.cut // 128), axis=1)
        return uv[rows, cols] * wide - uv[slice(d.rows + rows.start, d.rows + rows.stop), cols] * scale

    cuts = [slice(i * d.cut, (i + 1) * d.cut) for i in range(CUTS)]
    for i in range(CUTS):
        csend[i] = part(halves[1], cuts[i]).astype(BF16)
        send(csend.at[i], crecv.at[i], cs.at[i], cr.at[i], sibling)

    for i in range(CUTS):
        mine = part(halves[0], cuts[i])
        arrived(crecv.at[i], cr.at[i])
        mine = (mine + crecv[i].astype(F32)).astype(BF16).astype(F32)
        for h in range(d.chips):
            psend[i, h] = mine[h * d.qd : (h + 1) * d.qd].astype(BF16)
        precv[i, chip] = psend[i, chip]

        def give_back(k, _, i=i):
            h = (chip + k) % d.chips
            remote(psend.at[i, h], precv.at[i, chip], ps.at[i], pr.at[i], dev_chip(h)).start()
            return 0

        lax.fori_loop(1, d.chips, give_back, 0)

    losses = best + jnp.log(zs) - ds
    flat = iota((nr, 128), 0) * 128 + iota((nr, 128), 1)
    out = jnp.zeros((1, 128), F32)
    for i in range(d.qd):
        value = jnp.sum(
            jnp.sum(jnp.where(flat == chip * d.qd + i, losses, 0.0), axis=0, keepdims=True),
            axis=1,
            keepdims=True,
        )
        out = jnp.where(iota((1, 128), 1) == i, value + entropy[i : i + 1], out)
    loss_ref[...] = out[:, : d.qd]

    for i in range(CUTS):
        arrived(precv.at[i, pl.ds(0, d.chips - 1)], pr.at[i])
        total = precv[i, 0].astype(F32)
        for h in range(1, d.chips):
            total = total + precv[i, h].astype(F32)
        grad_ref[:, cuts[i]] = total

    for copy in pending:
        copy.wait_send()
    sent(qrecv.at[pl.ds(0, d.chips - 1)], qs.at[0])
    for i in range(CUTS):
        sent(psend.at[i, pl.ds(0, d.chips - 1)], ps.at[i])


def per_device(n, queries, cache, cand_ids, owner_map, teacher_rank):
    d = Dims(n, queries.shape, cache.shape, cand_ids.shape)
    w = d.width
    nxc, nyz = 2 * n, n * n
    dma = lambda k: [pltpu.SemaphoreType.DMA((k,))] * 2
    vmem = pl.BlockSpec(memory_space=pltpu.VMEM)
    grad, loss = pl.pallas_call(
        functools.partial(kernel, d),
        out_shape=(
            jax.ShapeDtypeStruct((d.qd, w), F32),
            jax.ShapeDtypeStruct((1, d.qd), F32),
        ),
        in_specs=[vmem] * 4 + [pl.BlockSpec(memory_space=pl.ANY)],
        out_specs=(vmem, vmem),
        scratch_shapes=[
            pltpu.VMEM((d.held, w), BF16),
            pltpu.VMEM((d.qd, w), BF16),
            pltpu.VMEM((d.chips, d.qd, w), BF16),
            pltpu.VMEM((d.rows, w), BF16),
            pltpu.VMEM((d.devices, 128), F32),
            pltpu.VMEM((d.devices, 128), F32),
            pltpu.VMEM((d.devices, 128), F32),
            pltpu.VMEM((d.devices, 128), F32),
            pltpu.VMEM((5, d.groups, 128), F32),
            pltpu.VMEM((d.rows, d.held), F32),
            pltpu.VMEM((d.rows, d.held), F32),
            pltpu.VMEM((d.rows, d.held), F32),
            pltpu.VMEM((2 * d.rows, d.held), BF16),
            pltpu.VMEM((d.rows, 128), F32),
            pltpu.VMEM((d.rows, 128), F32),
            pltpu.VMEM((d.rows, 128), F32),
            pltpu.VMEM((16, 128), F32),
            pltpu.VMEM((nxc, 16, 128), F32),
            pltpu.VMEM((16, 128), F32),
            pltpu.VMEM((nyz, 16, 128), F32),
            pltpu.VMEM((2 * d.rows, w), F32),
            pltpu.VMEM((CUTS, d.half, d.cut), BF16),
            pltpu.VMEM((CUTS, d.half, d.cut), BF16),
            pltpu.VMEM((CUTS, d.chips, d.qd, d.cut), BF16),
            pltpu.VMEM((CUTS, d.chips, d.qd, d.cut), BF16),
            pltpu.SemaphoreType.DMA,
            pltpu.SemaphoreType.DMA((1,)),
            pltpu.SemaphoreType.DMA((n,)),
            *dma(n),
            *dma(nxc),
            *dma(nyz),
            *dma(nxc),
            *dma(nyz),
            *dma(CUTS),
            *dma(CUTS),
        ],
        compiler_params=pltpu.CompilerParams(
            collective_id=0, has_side_effects=True, vmem_limit_bytes=60 * 2**20
        ),
    )(queries, cand_ids, owner_map.reshape(-1, 128), teacher_rank, cache)
    return grad, loss.reshape(d.qd)


def solution(mesh):
    n = mesh.shape["grp"]
    both = P(("grp", "shard"), None)
    return jax.shard_map(
        functools.partial(per_device, n),
        mesh=mesh,
        in_specs=(both, both, both, P(), both),
        out_specs=(both, P(("grp", "shard"))),
        check_vma=False,
    )
```

time: 74.3 us -> 64.1 us (0.86)
  Pallas kernels: 70.9 us -> 60.8 us
    pallas_call x1, Pallas kernels: 70.9 us -> 60.8 us  [per_device(): pl.pallas_call(functools.partial(kernel, d), out_shape=(jax.ShapeDtypeStr...]
where the time goes in v2:
time: 64.1 us; the launch traced here: 63.9 us
  Pallas kernels  60.8 us (95%)
  local copies, waits for them, and re-layouts  2.46 us (4%)
    pallas_call x1, Pallas kernels, per_device(): pl.pallas_call(functools.partial(kernel, d), out_shape=(jax.ShapeDtypeStr...  60.8 us
    unnamed x2, local copies, waits for them, and re-layouts  2.46 us

profile of v2, /device:TPU:1, one launch (start us, length us, event | category | flops | bytes accessed | tf_op | source)
XLA Modules:
  0.0 63.9 jit_solution(809627193557557776)
XLA Ops:
  0.6 60.8 %shard_map.68 = (f32[4,1024]{1,0:T(4,128)}, f32[1,4]{1,0:T(1,128)}) custom-call(f32[4,1024]{1,0:T(4,128)} %q_ref.1, s32[4,256]{1,0:T(4,128)} %cand_ref.1, s32[32,128]{1,0:T(8,128)} %bitcast.2, s32[4,256]{1,0:T(4,128)} %rank_ref.1, bf16[4096,1024]{1,0:T(8,128)(2,1)} %cache_hbm.1), custom_call_target="tpu_custom_call" | custom-call | tf_op jit(solution)/shard_map/pallas_call | solution.py:496
  61.4 1.3 %copy.9 = f32[4,1024]{1,0:T(4,128)} copy(f32[4,1024]{1,0:T(4,128)} %get-tuple-element.8) | data formatting | bytes 32768
  62.7 1.1 %copy.10 = f32[4]{0:T(128)} copy(f32[4]{0:T(128)} %bitcast.3) | data formatting | bytes 32

commit v3 on v2

--- a/solution.py
+++ b/solution.py
@@ -126,35 +126,35 @@
     n = d.n
     z = lax.axis_index("grp")
     shard = lax.axis_index("shard")
-    x = shard // (2 * n)
-    y = (shard // 2) % n
-    c = shard % 2
+    x = lax.div(shard, 2 * n)
+    y = lax.rem(lax.div(shard, 2), n)
+    c = lax.rem(shard, 2)
     scale = 3.0 / math.sqrt(d.width)
     xc = x * 2 + c
     yz = y * n + z
-    chip = z * d.layer + shard // 2
+    chip = z * d.layer + lax.div(shard, 2)
     nxc, nyz = 2 * n, n * n
 
     def dev(xx, yy, zz, cc):
         return (zz, (xx * n + yy) * 2 + cc)
 
     def dev_xc(j):
-        return dev(j // 2, y, z, j % 2)
+        return dev(lax.div(j, 2), y, z, lax.rem(j, 2))
 
     def dev_yz(j):
-        return dev(x, j // n, j % n, c)
-
-    def dev_chip(h):
-        return (h // d.layer, (h % d.layer) * 2 + c)
+        return dev(x, lax.div(j, n), lax.rem(j, n), c)
+
+    def other(k):
+        h = lax.rem(chip + k, d.chips)
+        return (lax.div(h, d.layer), lax.rem(h, d.layer) * 2 + c), h
 
     sibling = dev(x, y, z, 1 - c)
 
     barrier = pltpu.get_barrier_semaphore()
 
     def greet(k, _):
-        pl.semaphore_signal(
-            barrier, inc=1, device_id=dev_chip((chip + k) % d.chips), device_id_type=MESH
-        )
+        to, _ = other(k)
+        pl.semaphore_signal(barrier, inc=1, device_id=to, device_id_type=MESH)
         return 0
 
     lax.fori_loop(1, d.chips, greet, 0)
@@ -162,7 +162,7 @@
     for k in range(1, nxc):
         if k % 2:
             other_core += 1
-            pl.semaphore_signal(barrier, inc=1, device_id=dev_xc((xc + k) % nxc), device_id_type=MESH)
+            pl.semaphore_signal(barrier, inc=1, device_id=dev_xc(lax.rem(xc + k, nxc)), device_id_type=MESH)
 
     cache_copy = pltpu.make_async_copy(cache_hbm, c_ref, cache_sem)
     cache_copy.start()
@@ -240,7 +240,7 @@
     pl.semaphore_wait(barrier, d.chips - 1 + other_core)
 
     for k in range(1, nxc):
-        j = (xc + k) % nxc
+        j = lax.rem(xc + k, nxc)
         send(
             table.at[pl.ds(pl.multiple_of(j * nyz, nyz), nyz)],
             ra.at[pl.ds(pl.multiple_of(xc * nyz, nyz), nyz)],
@@ -250,21 +250,22 @@
         )
 
     def give(k, _):
-        remote(qown, qrecv.at[chip], qs.at[0], qr.at[z], dev_chip((chip + k) % d.chips)).start()
+        to, _ = other(k)
+        remote(qown, qrecv.at[chip], qs.at[0], qr.at[z], to).start()
         return 0
 
     lax.fori_loop(1, d.chips, give, 0)
     own = pl.ds(pl.multiple_of(xc * nyz, nyz), nyz)
     ra[own] = table[own]
     for k in range(1, nxc):
-        src = (xc + nxc - k) % nxc
+        src = lax.rem(xc + nxc - k, nxc)
         arrived(ra.at[pl.ds(pl.multiple_of(src * nyz, nyz), nyz)], tar.at[k])
 
     r, s = iota((d.devices, d.devices), 0), iota((d.devices, d.devices), 1)
     perm = hot((r % nxc) * nyz + r // nxc == s)
     ra2[...] = nn(perm, ra[...].astype(BF16))
     for k in range(1, nyz):
-        j = (yz + k) % nyz
+        j = lax.rem(yz + k, nyz)
         send(
             ra2.at[pl.ds(pl.multiple_of(j * nxc, nxc), nxc)],
             rb.at[pl.ds(pl.multiple_of(yz * nxc, nxc), nxc)],
@@ -274,8 +275,28 @@
         )
     own = pl.ds(pl.multiple_of(yz * nxc, nxc), nxc)
     rb[own] = ra2[own]
+
+    per = max(1, 16 // d.qd)
+    for k in range(n):
+        layer = lax.rem(z + k, n)
+        count = d.layer - 1 if k == 0 else d.layer
+        arrived(qrecv.at[pl.ds(layer * d.layer, count)], qr.at[layer])
+
+        def place(i, _, layer=layer):
+            first = layer * d.layer + i * per
+            rows = [qrecv[first + j].astype(F32) for j in range(per)]
+            at = pl.multiple_of(first * d.qd, per * d.qd)
+            qall[pl.ds(at, per * d.qd)] = jnp.concatenate(rows, axis=0).astype(BF16)
+            return 0
+
+        lax.fori_loop(0, d.layer // per, place, 0)
+        size = d.layer * d.qd
+        here = pl.ds(pl.multiple_of(layer * size, size), size)
+        there = pl.ds(pl.multiple_of(d.half + layer * size, size), size)
+        send(qall.at[here], qall.at[there], xs.at[k], xr.at[layer], sibling)
+
     for k in range(1, nyz):
-        src = (yz + nyz - k) % nyz
+        src = lax.rem(yz + nyz - k, nyz)
         arrived(rb.at[pl.ds(pl.multiple_of(src * nxc, nxc), nxc)], tbr.at[k])
 
     rc = jnp.where(r < d.chips, c, 1 - c)
@@ -315,21 +336,8 @@
                 et[pl.ds(pl.multiple_of(d.rows + g * d.grows, d.grows), d.grows), cols] = tp.astype(BF16)
         return 0
 
-    lax.fori_loop(0, d.groups, fill, 0)
-
-    per = max(1, 16 // d.qd)
-    for k in range(n):
-        layer = (z + k) % n
-        count = d.layer - 1 if k == 0 else d.layer
-        arrived(qrecv.at[pl.ds(layer * d.layer, count)], qr.at[layer])
-        for i in range(0, d.layer, per):
-            rows = [qrecv[layer * d.layer + i + j].astype(F32) for j in range(per)]
-            at = pl.multiple_of((layer * d.layer + i) * d.qd, per * d.qd)
-            qall[pl.ds(at, per * d.qd)] = jnp.concatenate(rows, axis=0).astype(BF16)
-        size = d.layer * d.qd
-        here = pl.ds(pl.multiple_of(layer * size, size), size)
-        there = pl.ds(pl.multiple_of(d.half + layer * size, size), size)
-        send(qall.at[here], qall.at[there], xs.at[k], xr.at[layer], sibling)
+    lax.fori_loop(0, d.groups, fill, 0, unroll=min(4, d.groups))
+
     cache_copy.wait()
     cache_waited = True
 
@@ -337,61 +345,59 @@
     zbuf[...] = jnp.zeros(zbuf.shape, F32)
     dbuf[...] = jnp.zeros(dbuf.shape, F32)
     halves = [slice(0, d.half), slice(d.half, d.rows)]
+    tiles = [slice(t, t + d.tile) for t in range(0, d.held, d.tile)]
+    step = min(64, d.half)
 
     def score(rows, cols):
-        raw = nt(qall[rows], c_ref[cols, :])
-        raw = jnp.where(nbuf[rows, cols] > 0.0, raw, NEG)
-        sbuf[rows, cols] = raw
-        best = mbuf[rows]
-        for k in range(d.tile // 128):
-            best = jnp.maximum(best, raw[:, k * 128 : (k + 1) * 128])
-        mbuf[rows] = best
-
-    def expo(rows, t):
-        step = min(64, d.half)
-        for r0 in range(rows.start, rows.stop, step):
-            rr = slice(r0, r0 + step)
-            top = mbuf[rr]
-            za, da = zbuf[rr], dbuf[rr]
-            for k in range(d.tile // 128):
-                cols = pl.ds(pl.multiple_of(t * d.tile + k * 128, 128), 128)
-                raw = sbuf[rr, cols]
-                e = nbuf[rr, cols] * jnp.exp((raw - top) * scale)
-                et[rr, cols] = e.astype(BF16)
-                za = za + e
-                da = da + tbuf[rr, cols] * raw
-            zbuf[rr], dbuf[rr] = za, da
+        sbuf[rows, cols] = nt(qall[rows], c_ref[cols])
+
+    def lanes(cols):
+        return [slice(k, k + 128) for k in range(cols.start, cols.stop, 128)]
+
+    def blocks(rows):
+        return [slice(r, r + step) for r in range(rows.start, rows.stop, step)]
+
+    def largest(rows, cols):
+        for rr in blocks(rows):
+            best, dot = mbuf[rr], dbuf[rr]
+            for cc in lanes(cols):
+                logits = sbuf[rr, cc] * scale
+                dot = dot + tbuf[rr, cc] * logits
+                best = jnp.maximum(best, jnp.where(nbuf[rr, cc] > 0.0, logits, NEG))
+            mbuf[rr] = best
+            dbuf[rr] = dot
 
     def widest(rows):
         mbuf[rows] = jnp.broadcast_to(jnp.max(mbuf[rows], axis=1, keepdims=True), (d.half, 128))
 
-    def tiles(body):
-        def step(t, _):
-            body(t, pl.ds(pl.multiple_of(t * d.tile, d.tile), d.tile))
-            return 0
-
-        lax.fori_loop(0, d.held // d.tile, step, 0)
-
-    tiles(lambda t, cols: score(halves[0], cols))
-    widest(halves[0])
-    for layer in range(n):
-        size = d.layer * d.qd
-        arrived(qall.at[pl.ds(d.half + layer * size, size)], xr.at[layer])
-
-    def both(t, cols):
-        score(halves[1], cols)
-        expo(halves[0], t)
-
-    tiles(both)
-    widest(halves[1])
-    tiles(lambda t, cols: expo(halves[1], t))
+    def expo(rows, cols):
+        for rr in blocks(rows):
+            top, total = mbuf[rr], zbuf[rr]
+            for cc in lanes(cols):
+                e = nbuf[rr, cc] * jnp.exp(jnp.minimum(sbuf[rr, cc] * scale - top, 0.0))
+                et[rr, cc] = e.astype(BF16)
+                total = total + e
+            zbuf[rr] = total
+
+    for h in range(2):
+        if h == 1:
+            for layer in range(n):
+                size = d.layer * d.qd
+                arrived(qall.at[pl.ds(d.half + layer * size, size)], xr.at[layer])
+        for cols in tiles:
+            score(halves[h], cols)
+        for cols in tiles:
+            largest(halves[h], cols)
+        widest(halves[h])
+        for cols in tiles:
+            expo(halves[h], cols)
 
     nr = d.stat_rows
-    my_top = col_to_rows(mbuf[:, :1]) * scale
+    my_top = col_to_rows(mbuf[:, :1])
     packed = [
         my_top,
         col_to_rows(jnp.sum(zbuf[...], axis=1, keepdims=True)),
-        col_to_rows(jnp.sum(dbuf[...], axis=1, keepdims=True)) * scale,
+        col_to_rows(jnp.sum(dbuf[...], axis=1, keepdims=True)),
     ]
     spare = [jnp.zeros((16 - 3 * nr, 128), F32)] if 16 - 3 * nr else []
     stat[...] = jnp.concatenate(packed + spare, axis=0)
@@ -410,16 +416,14 @@
         return [v[:nr], v[nr : 2 * nr], v[2 * nr : 3 * nr]]
 
     for k in range(1, nxc):
-        send(stat, sa.at[k], sas.at[k], sar.at[k], dev_xc((xc + k) % nxc))
-
-    uv_cols = 256
+        send(stat, sa.at[k], sas.at[k], sar.at[k], dev_xc(lax.rem(xc + k, nxc)))
 
     def product(t, _):
-        cols = pl.ds(pl.multiple_of(t * uv_cols, uv_cols), uv_cols)
+        cols = pl.ds(pl.multiple_of(t * 256, 256), 256)
         uv[:, cols] = nn(et[...], c_ref[:, cols])
         return 0
 
-    steps = d.width // uv_cols
+    steps = d.width // 256
     lax.fori_loop(0, steps // 2, product, 0)
     for k in range(1, nxc):
         arrived(sa.at[k], sar.at[k])
@@ -429,7 +433,7 @@
         pieces.append([swap(v) for v in got] if k % 2 else got)
     stat2[...] = jnp.concatenate(list(combine(pieces)) + spare, axis=0)
     for k in range(1, nyz):
-        send(stat2, sb.at[k], sbs.at[k], sbr.at[k], dev_yz((yz + k) % nyz))
+        send(stat2, sb.at[k], sbs.at[k], sbr.at[k], dev_yz(lax.rem(yz + k, nyz)))
     lax.fori_loop(steps // 2, steps, product, 0)
     for k in range(1, nyz):
         arrived(sb.at[k], sbr.at[k])
@@ -449,14 +453,21 @@
     for i in range(CUTS):
         mine = part(halves[0], cuts[i])
         arrived(crecv.at[i], cr.at[i])
-        mine = (mine + crecv[i].astype(F32)).astype(BF16).astype(F32)
-        for h in range(d.chips):
-            psend[i, h] = mine[h * d.qd : (h + 1) * d.qd].astype(BF16)
+        uv[halves[0], cuts[i]] = mine + crecv[i].astype(F32)
+        size = max(8, d.qd)
+
+        def split(j, _, i=i):
+            rows = uv[pl.ds(pl.multiple_of(j * size, size), size), cuts[i]]
+            for k in range(size // d.qd):
+                psend[i, j * (size // d.qd) + k] = rows[k * d.qd : (k + 1) * d.qd].astype(BF16)
+            return 0
+
+        lax.fori_loop(0, d.half // size, split, 0, unroll=4)
         precv[i, chip] = psend[i, chip]
 
         def give_back(k, _, i=i):
-            h = (chip + k) % d.chips
-            remote(psend.at[i, h], precv.at[i, chip], ps.at[i], pr.at[i], dev_chip(h)).start()
+            to, h = other(k)
+            remote(psend.at[i, h], precv.at[i, chip], ps.at[i], pr.at[i], to).start()
             return 0
 
         lax.fori_loop(1, d.chips, give_back, 0)
@@ -475,16 +486,24 @@
 
     for i in range(CUTS):
         arrived(precv.at[i, pl.ds(0, d.chips - 1)], pr.at[i])
-        total = precv[i, 0].astype(F32)
-        for h in range(1, d.chips):
-            total = total + precv[i, h].astype(F32)
-        grad_ref[:, cuts[i]] = total
+        grad_ref[:, cuts[i]] = lax.fori_loop(
+            0,
+            d.chips,
+            lambda h, total, i=i: total + precv[i, h].astype(F32),
+            jnp.zeros((d.qd, d.cut), F32),
+            unroll=8,
+        )
 
     for copy in pending:
         copy.wait_send()
     sent(qrecv.at[pl.ds(0, d.chips - 1)], qs.at[0])
     for i in range(CUTS):
         sent(psend.at[i, pl.ds(0, d.chips - 1)], ps.at[i])
+
+
+def hand_over(grad_ref, loss_ref, grad_out, loss_out):
+    grad_out[...] = grad_ref[...]
+    loss_out[...] = loss_ref[...]
 
 
 def per_device(n, queries, cache, cand_ids, owner_map, teacher_rank):
@@ -542,6 +561,15 @@
             collective_id=0, has_side_effects=True, vmem_limit_bytes=60 * 2**20
         ),
     )(queries, cand_ids, owner_map.reshape(-1, 128), teacher_rank, cache)
+    grad, loss = pl.pallas_call(
+        hand_over,
+        out_shape=(
+            jax.ShapeDtypeStruct((d.qd, w), F32),
+            jax.ShapeDtypeStruct((1, d.qd), F32),
+        ),
+        in_specs=[vmem] * 2,
+        out_specs=(vmem, vmem),
+    )(grad, loss)
     return grad, loss.reshape(d.qd)
 
 

time: 64.1 us -> 58.1 us (0.906)
  Pallas kernels: 60.8 us -> 57.2 us
  local copies, waits for them, and re-layouts: 2.46 us -> 0 us
    pallas_call x1, Pallas kernels: 60.8 us -> 55.9 us  [per_device(): pl.pallas_call(functools.partial(kernel, d), out_shape=(jax.ShapeDtypeStr...]
    unnamed x2 -> x0, local copies, waits for them, and re-layouts: 2.46 us -> none
    pallas_call x0 -> x1, Pallas kernels: none -> 1.33 us  [per_device(): pl.pallas_call(hand_over, out_shape=(jax.ShapeDtypeStruct((d.qd, w), F32)...]
where the time goes in v3:
time: 58.1 us; the launch traced here: 57.9 us
  Pallas kernels  57.2 us (98%)
  between operations  0.64 us (1%)
    pallas_call x1, Pallas kernels, per_device(): pl.pallas_call(functools.partial(kernel, d), out_shape=(jax.ShapeDtypeStr...  55.9 us
    pallas_call x1, Pallas kernels, per_device(): pl.pallas_call(hand_over, out_shape=(jax.ShapeDtypeStruct((d.qd, w), F32)...  1.33 us

profile of v3, /device:TPU:1, one launch (start us, length us, event | category | flops | bytes accessed | tf_op | source)
XLA Modules:
  0.0 57.9 jit_solution(17803132594438331829)
XLA Ops:
  0.6 55.9 %shard_map.68 = (f32[4,1024]{1,0:T(4,128)}, f32[1,4]{1,0:T(1,128)}) custom-call(f32[4,1024]{1,0:T(4,128)} %q_ref.1, s32[4,256]{1,0:T(4,128)} %cand_ref.1, s32[32,128]{1,0:T(8,128)} %bitcast.2, s32[4,256]{1,0:T(4,128)} %rank_ref.1, bf16[4096,1024]{1,0:T(8,128)(2,1)} %cache_hbm.1), custom_call_target="tpu_custom_call" | custom-call | tf_op jit(solution)/shard_map/pallas_call | solution.py:515
  56.5 1.3 %shard_map.69 = (f32[4,1024]{1,0:T(4,128)}, f32[1,4]{1,0:T(1,128)}) custom-call(f32[4,1024]{1,0:T(4,128)} %get-tuple-element.6.grad_ref, f32[1,4]{1,0:T(1,128)} %get-tuple-element.7.loss_ref), custom_call_target="tpu_custom_call" | custom-call | tf_op jit(solution)/shard_map/pallas_call | solution.py:564

commit v4 on v3

--- a/solution.py
+++ b/solution.py
@@ -73,13 +73,17 @@
 
 def kernel(
     d,
+    q_hbm,
+    cand_hbm,
+    map_hbm,
+    rank_hbm,
+    cache_hbm,
+    grad_ref,
+    loss_ref,
     q_ref,
     cand_ref,
     map_ref,
     rank_ref,
-    cache_hbm,
-    grad_ref,
-    loss_ref,
     c_ref,
     qown,
     qrecv,
@@ -105,6 +109,7 @@
     crecv,
     psend,
     precv,
+    small_sem,
     cache_sem,
     qs,
     qr,
@@ -144,11 +149,34 @@
     def dev_yz(j):
         return dev(x, lax.div(j, n), lax.rem(j, n), c)
 
+    away = sorted(range(n), key=lambda v: -min(v, n - v))
+
+    def ahead(at, t):
+        by = away[-1]
+        for i in range(n - 1):
+            by = jnp.where(t == i, away[i], by)
+        return lax.rem(at + by, n)
+
     def other(k):
-        h = lax.rem(chip + k, d.chips)
-        return (lax.div(h, d.layer), lax.rem(h, d.layer) * 2 + c), h
+        zz = ahead(z, lax.div(k, d.layer))
+        xx = ahead(x, lax.rem(lax.div(k, n), n))
+        yy = ahead(y, lax.rem(k, n))
+        h = xx * n + yy
+        return (zz, h * 2 + c), zz * d.layer + h
+
+    far_xc = sorted(range(1, nxc), key=lambda k: -min(k, nxc - k))
+    far_yz = sorted(range(1, nyz), key=lambda k: -min(k // n, n - k // n) - min(k % n, n - k % n))
 
     sibling = dev(x, y, z, 1 - c)
+
+    small = [
+        pltpu.make_async_copy(src, dst, small_sem.at[i])
+        for i, (src, dst) in enumerate(
+            [(cand_hbm, cand_ref), (map_hbm, map_ref), (rank_hbm, rank_ref), (q_hbm, q_ref)]
+        )
+    ]
+    for copy in small:
+        copy.start()
 
     barrier = pltpu.get_barrier_semaphore()
 
@@ -157,7 +185,7 @@
         pl.semaphore_signal(barrier, inc=1, device_id=to, device_id_type=MESH)
         return 0
 
-    lax.fori_loop(1, d.chips, greet, 0)
+    lax.fori_loop(0, d.chips - 1, greet, 0)
     other_core = 0
     for k in range(1, nxc):
         if k % 2:
@@ -185,6 +213,8 @@
     def sent(src, ssem):
         remote(src, src, ssem, ssem, sibling).wait_send()
 
+    for copy in small:
+        copy.wait()
     q16 = q_ref[...].astype(BF16)
     qown[...] = q16
     qrecv[chip] = q16
@@ -215,8 +245,7 @@
             + jnp.sum(got[map_rows:] * high, axis=0, keepdims=True)
         ).astype(I32)
         owner, lblk = pblk // d.blocks, pblk % d.blocks
-        oz, oshard = owner // (2 * n * n), owner % (2 * n * n)
-        place = ((oshard // (2 * n)) * 2 + oshard % 2) * nyz + ((oshard // 2) % n) * n + oz
+        place = (owner % 2) * d.chips + owner // 2
         mine = jnp.where(iota((d.devices, d.cands), 0) == place, 1.0, 0.0)
         mine16 = mine.astype(BF16)
         earlier = nn(mine16, upper) + total
@@ -235,75 +264,32 @@
             axis=0,
         ).astype(BF16)
         acc = acc + nt(mine16, planes)
-    table[...] = acc
+    for core in range(2):
+        table[:, core, :] = acc[core * d.chips : (core + 1) * d.chips]
+    ra[chip] = table[chip]
 
     pl.semaphore_wait(barrier, d.chips - 1 + other_core)
 
-    for k in range(1, nxc):
-        j = lax.rem(xc + k, nxc)
-        send(
-            table.at[pl.ds(pl.multiple_of(j * nyz, nyz), nyz)],
-            ra.at[pl.ds(pl.multiple_of(xc * nyz, nyz), nyz)],
-            tas.at[k],
-            tar.at[k],
-            dev_xc(j),
-        )
+    def ask(k, _):
+        to, h = other(k)
+        remote(table.at[h], ra.at[chip], tas.at[0], tar.at[0], to).start()
+        return 0
+
+    lax.fori_loop(0, d.chips - 1, ask, 0)
 
     def give(k, _):
         to, _ = other(k)
         remote(qown, qrecv.at[chip], qs.at[0], qr.at[z], to).start()
         return 0
 
-    lax.fori_loop(1, d.chips, give, 0)
-    own = pl.ds(pl.multiple_of(xc * nyz, nyz), nyz)
-    ra[own] = table[own]
-    for k in range(1, nxc):
-        src = lax.rem(xc + nxc - k, nxc)
-        arrived(ra.at[pl.ds(pl.multiple_of(src * nyz, nyz), nyz)], tar.at[k])
-
-    r, s = iota((d.devices, d.devices), 0), iota((d.devices, d.devices), 1)
-    perm = hot((r % nxc) * nyz + r // nxc == s)
-    ra2[...] = nn(perm, ra[...].astype(BF16))
-    for k in range(1, nyz):
-        j = lax.rem(yz + k, nyz)
-        send(
-            ra2.at[pl.ds(pl.multiple_of(j * nxc, nxc), nxc)],
-            rb.at[pl.ds(pl.multiple_of(yz * nxc, nxc), nxc)],
-            tbs.at[k],
-            tbr.at[k],
-            dev_yz(j),
-        )
-    own = pl.ds(pl.multiple_of(yz * nxc, nxc), nxc)
-    rb[own] = ra2[own]
-
-    per = max(1, 16 // d.qd)
-    for k in range(n):
-        layer = lax.rem(z + k, n)
-        count = d.layer - 1 if k == 0 else d.layer
-        arrived(qrecv.at[pl.ds(layer * d.layer, count)], qr.at[layer])
-
-        def place(i, _, layer=layer):
-            first = layer * d.layer + i * per
-            rows = [qrecv[first + j].astype(F32) for j in range(per)]
-            at = pl.multiple_of(first * d.qd, per * d.qd)
-            qall[pl.ds(at, per * d.qd)] = jnp.concatenate(rows, axis=0).astype(BF16)
-            return 0
-
-        lax.fori_loop(0, d.layer // per, place, 0)
-        size = d.layer * d.qd
-        here = pl.ds(pl.multiple_of(layer * size, size), size)
-        there = pl.ds(pl.multiple_of(d.half + layer * size, size), size)
-        send(qall.at[here], qall.at[there], xs.at[k], xr.at[layer], sibling)
-
-    for k in range(1, nyz):
-        src = lax.rem(yz + nyz - k, nyz)
-        arrived(rb.at[pl.ds(pl.multiple_of(src * nxc, nxc), nxc)], tbr.at[k])
-
-    rc = jnp.where(r < d.chips, c, 1 - c)
-    rh = r % d.chips
-    rz, rx, ry = rh // d.layer, (rh // n) % n, rh % n
-    perm = hot(((ry * n + rz) * n + rx) * 2 + rc == s)
-    lists = nn(perm, rb[...].astype(BF16)).astype(BF16)
+    lax.fori_loop(0, d.chips - 1, give, 0)
+    arrived(ra.at[pl.ds(0, d.chips - 1)], tar.at[0])
+    pair = [ra[:, core, :] for core in range(2)]
+    ra2[...] = jnp.where(c == 0, pair[1], pair[0])
+    send(ra2, rb.at[pl.ds(d.chips, d.chips)], tbs.at[0], tbr.at[0], sibling)
+    rb[: d.chips] = jnp.where(c == 0, pair[0], pair[1])
+    arrived(rb.at[pl.ds(d.chips, d.chips)], tbr.at[0])
+    lists = rb[...].astype(BF16)
     lane = iota((128, 128), 1)
     sub = iota((128, 128), 0)
     pick = jnp.where(iota((d.devices, 128), 0) % 8 == iota((d.devices, 128), 1) // CAP, 1.0, 0.0)
@@ -336,7 +322,26 @@
                 et[pl.ds(pl.multiple_of(d.rows + g * d.grows, d.grows), d.grows), cols] = tp.astype(BF16)
         return 0
 
-    lax.fori_loop(0, d.groups, fill, 0, unroll=min(4, d.groups))
+    lax.fori_loop(0, d.groups, fill, 0, unroll=min(8, d.groups))
+
+    per = max(1, 16 // d.qd)
+    for k in range(n):
+        layer = lax.rem(z + k, n)
+        count = d.layer - 1 if k == 0 else d.layer
+        arrived(qrecv.at[pl.ds(layer * d.layer, count)], qr.at[layer])
+
+        def place(i, _, layer=layer):
+            first = layer * d.layer + i * per
+            rows = [qrecv[first + j].astype(F32) for j in range(per)]
+            at = pl.multiple_of(first * d.qd, per * d.qd)
+            qall[pl.ds(at, per * d.qd)] = jnp.concatenate(rows, axis=0).astype(BF16)
+            return 0
+
+        lax.fori_loop(0, d.layer // per, place, 0, unroll=True)
+        size = d.layer * d.qd
+        here = pl.ds(pl.multiple_of(layer * size, size), size)
+        there = pl.ds(pl.multiple_of(d.half + layer * size, size), size)
+        send(qall.at[here], qall.at[there], xs.at[k], xr.at[layer], sibling)
 
     cache_copy.wait()
     cache_waited = True
@@ -415,7 +420,7 @@
     def three(v):
         return [v[:nr], v[nr : 2 * nr], v[2 * nr : 3 * nr]]
 
-    for k in range(1, nxc):
+    for k in far_xc:
         send(stat, sa.at[k], sas.at[k], sar.at[k], dev_xc(lax.rem(xc + k, nxc)))
 
     def product(t, _):
@@ -432,7 +437,7 @@
         got = three(sa[k])
         pieces.append([swap(v) for v in got] if k % 2 else got)
     stat2[...] = jnp.concatenate(list(combine(pieces)) + spare, axis=0)
-    for k in range(1, nyz):
+    for k in far_yz:
         send(stat2, sb.at[k], sbs.at[k], sbr.at[k], dev_yz(lax.rem(yz + k, nyz)))
     lax.fori_loop(steps // 2, steps, product, 0)
     for k in range(1, nyz):
@@ -470,7 +475,7 @@
             remote(psend.at[i, h], precv.at[i, chip], ps.at[i], pr.at[i], to).start()
             return 0
 
-        lax.fori_loop(1, d.chips, give_back, 0)
+        lax.fori_loop(0, d.chips - 1, give_back, 0)
 
     losses = best + jnp.log(zs) - ds
     flat = iota((nr, 128), 0) * 128 + iota((nr, 128), 1)
@@ -497,6 +502,7 @@
     for copy in pending:
         copy.wait_send()
     sent(qrecv.at[pl.ds(0, d.chips - 1)], qs.at[0])
+    sent(ra.at[pl.ds(0, d.chips - 1)], tas.at[0])
     for i in range(CUTS):
         sent(psend.at[i, pl.ds(0, d.chips - 1)], ps.at[i])
 
@@ -518,16 +524,20 @@
             jax.ShapeDtypeStruct((d.qd, w), F32),
             jax.ShapeDtypeStruct((1, d.qd), F32),
         ),
-        in_specs=[vmem] * 4 + [pl.BlockSpec(memory_space=pl.ANY)],
+        in_specs=[pl.BlockSpec(memory_space=pl.ANY)] * 5,
         out_specs=(vmem, vmem),
         scratch_shapes=[
+            pltpu.VMEM((d.qd, w), F32),
+            pltpu.VMEM((d.qd, d.cands), I32),
+            pltpu.VMEM((owner_map.shape[0] // 128, 128), I32),
+            pltpu.VMEM((d.qd, d.cands), I32),
             pltpu.VMEM((d.held, w), BF16),
             pltpu.VMEM((d.qd, w), BF16),
             pltpu.VMEM((d.chips, d.qd, w), BF16),
             pltpu.VMEM((d.rows, w), BF16),
-            pltpu.VMEM((d.devices, 128), F32),
-            pltpu.VMEM((d.devices, 128), F32),
-            pltpu.VMEM((d.devices, 128), F32),
+            pltpu.VMEM((d.chips, 2, 128), F32),
+            pltpu.VMEM((d.chips, 2, 128), F32),
+            pltpu.VMEM((d.chips, 128), F32),
             pltpu.VMEM((d.devices, 128), F32),
             pltpu.VMEM((5, d.groups, 128), F32),
             pltpu.VMEM((d.rows, d.held), F32),
@@ -546,12 +556,13 @@
             pltpu.VMEM((CUTS, d.half, d.cut), BF16),
             pltpu.VMEM((CUTS, d.chips, d.qd, d.cut), BF16),
             pltpu.VMEM((CUTS, d.chips, d.qd, d.cut), BF16),
+            pltpu.SemaphoreType.DMA((4,)),
             pltpu.SemaphoreType.DMA,
             pltpu.SemaphoreType.DMA((1,)),
             pltpu.SemaphoreType.DMA((n,)),
             *dma(n),
-            *dma(nxc),
-            *dma(nyz),
+            *dma(1),
+            *dma(1),
             *dma(nxc),
             *dma(nyz),
             *dma(CUTS),

time: 58.1 us -> 53.3 us (0.917)
  Pallas kernels: 57.2 us -> 52.4 us
    pallas_call x1, Pallas kernels: 55.9 us -> 51.1 us  [per_device(): pl.pallas_call(functools.partial(kernel, d), out_shape=(jax.ShapeDtypeStr...]
where the time goes in v4:
time: 53.3 us; the launch traced here: 53.1 us
  Pallas kernels  52.4 us (98%)
  between operations  0.64 us (1%)
    pallas_call x1, Pallas kernels, per_device(): pl.pallas_call(functools.partial(kernel, d), out_shape=(jax.ShapeDtypeStr...  51.1 us
    pallas_call x1, Pallas kernels, per_device(): pl.pallas_call(hand_over, out_shape=(jax.ShapeDtypeStruct((d.qd, w), F32)...  1.33 us

profile of v4, /device:TPU:1, one launch (start us, length us, event | category | flops | bytes accessed | tf_op | source)
XLA Modules:
  0.0 53.1 jit_solution(7356258010670327022)
XLA Ops:
  0.6 51.1 %shard_map.68 = (f32[4,1024]{1,0:T(4,128)}, f32[1,4]{1,0:T(1,128)}) custom-call(f32[4,1024]{1,0:T(4,128)} %q_hbm.1, s32[4,256]{1,0:T(4,128)} %cand_hbm.1, s32[32,128]{1,0:T(8,128)} %bitcast.2, s32[4,256]{1,0:T(4,128)} %rank_hbm.1, bf16[4096,1024]{1,0:T(8,128)(2,1)} %cache_hbm.1), custom_call_target="tpu_custom_call" | custom-call | tf_op jit(solution)/shard_map/pallas_call | solution.py:521
  51.7 1.3 %shard_map.69 = (f32[4,1024]{1,0:T(4,128)}, f32[1,4]{1,0:T(1,128)}) custom-call(f32[4,1024]{1,0:T(4,128)} %get-tuple-element.6.grad_ref, f32[1,4]{1,0:T(1,128)} %get-tuple-element.7.loss_ref), custom_call_target="tpu_custom_call" | custom-call | tf_op jit(solution)/shard_map/pallas_call | solution.py:575

commit v5 on v4

--- a/solution.py
+++ b/solution.py
@@ -282,7 +282,7 @@
         remote(qown, qrecv.at[chip], qs.at[0], qr.at[z], to).start()
         return 0
 
-    lax.fori_loop(0, d.chips - 1, give, 0)
+    lax.fori_loop(0, d.chips - 1, give, 0, unroll=3)
     arrived(ra.at[pl.ds(0, d.chips - 1)], tar.at[0])
     pair = [ra[:, core, :] for core in range(2)]
     ra2[...] = jnp.where(c == 0, pair[1], pair[0])
@@ -423,13 +423,10 @@
     for k in far_xc:
         send(stat, sa.at[k], sas.at[k], sar.at[k], dev_xc(lax.rem(xc + k, nxc)))
 
-    def product(t, _):
-        cols = pl.ds(pl.multiple_of(t * 256, 256), 256)
-        uv[:, cols] = nn(et[...], c_ref[:, cols])
-        return 0
-
-    steps = d.width // 256
-    lax.fori_loop(0, steps // 2, product, 0)
+    def product(rows):
+        uv[rows] = nn(et[rows], c_ref[...])
+
+    product(slice(0, d.rows))
     for k in range(1, nxc):
         arrived(sa.at[k], sar.at[k])
     pieces = [three(stat[...])]
@@ -439,7 +436,7 @@
     stat2[...] = jnp.concatenate(list(combine(pieces)) + spare, axis=0)
     for k in far_yz:
         send(stat2, sb.at[k], sbs.at[k], sbr.at[k], dev_yz(lax.rem(yz + k, nyz)))
-    lax.fori_loop(steps // 2, steps, product, 0)
+    product(slice(d.rows, 2 * d.rows))
     for k in range(1, nyz):
         arrived(sb.at[k], sbr.at[k])
     best, zs, ds = combine([three(stat2[...])] + [three(sb[k]) for k in range(1, nyz)])
@@ -475,7 +472,7 @@
             remote(psend.at[i, h], precv.at[i, chip], ps.at[i], pr.at[i], to).start()
             return 0
 
-        lax.fori_loop(0, d.chips - 1, give_back, 0)
+        lax.fori_loop(0, d.chips - 1, give_back, 0, unroll=3)
 
     losses = best + jnp.log(zs) - ds
     flat = iota((nr, 128), 0) * 128 + iota((nr, 128), 1)

time: 53.3 us -> 53 us (level)
  no operation moved by 1% of the time
where the time goes in v5:
time: 53 us; the launch traced here: 52.8 us
  Pallas kernels  52.2 us (98%)
  between operations  0.64 us (1%)
    pallas_call x1, Pallas kernels, per_device(): pl.pallas_call(functools.partial(kernel, d), out_shape=(jax.ShapeDtypeStr...  50.9 us
    pallas_call x1, Pallas kernels, per_device(): pl.pallas_call(hand_over, out_shape=(jax.ShapeDtypeStruct((d.qd, w), F32)...  1.33 us

profile of v5, /device:TPU:1, one launch (start us, length us, event | category | flops | bytes accessed | tf_op | source)
XLA Modules:
  0.0 52.8 jit_solution(10023606278532902897)
XLA Ops:
  0.6 50.9 %shard_map.68 = (f32[4,1024]{1,0:T(4,128)}, f32[1,4]{1,0:T(1,128)}) custom-call(f32[4,1024]{1,0:T(4,128)} %q_hbm.1, s32[4,256]{1,0:T(4,128)} %cand_hbm.1, s32[32,128]{1,0:T(8,128)} %bitcast.2, s32[4,256]{1,0:T(4,128)} %rank_hbm.1, bf16[4096,1024]{1,0:T(8,128)(2,1)} %cache_hbm.1), custom_call_target="tpu_custom_call" | custom-call | tf_op jit(solution)/shard_map/pallas_call | solution.py:518
  51.5 1.3 %shard_map.69 = (f32[4,1024]{1,0:T(4,128)}, f32[1,4]{1,0:T(1,128)}) custom-call(f32[4,1024]{1,0:T(4,128)} %get-tuple-element.6.grad_ref, f32[1,4]{1,0:T(1,128)} %get-tuple-element.7.loss_ref), custom_call_target="tpu_custom_call" | custom-call | tf_op jit(solution)/shard_map/pallas_call | solution.py:572
